TPU v7x, 32 devices: a whole 2x2x4 slice. The times are simulated.
32 devices in a mesh: shard: 8 (over z, core), ctx: 2 (over x), tp: 2 (over y).
Axes of the slice: x: 2, y: 2, z: 4, core: 2. Of those that a mesh axis runs over, the one named last changes fastest.
Arguments:
- tokens: bfloat16 [16, 1032, 1024], P('shard', 'ctx'), may hold values from -6 to 6
- cotangent: bfloat16 [16, 1032, 1024], P('shard', 'ctx'), may hold values from -6 to 6
- valid_tokens: int32 [16, 1032], P('shard'), may hold values from 0 to 1, as said below
- places: int32 [2, 16, 1032], P(None, 'shard', 'ctx'), may hold values from 0 to 31, as said below
- qkv_weight: bfloat16 [3, 1024, 1024], P(None, 'shard', 'tp'), may hold values from -0.1875 to 0.1875
- head_biases: bfloat16 [3, 16, 64], P(None, 'tp', 'shard'), may hold values from -1.1953125 to 1.1953125
- head_gain: bfloat16 [16, 64], P('tp', 'shard'), may hold values from 0.5 to 1.5
- out_weight: bfloat16 [1024, 1024], P('tp', 'shard'), may hold values from -0.1875 to 0.1875
- norm_gains: bfloat16 [2, 1024], P(None, 'shard'), may hold values from 0.5 to 1.5
- width_biases: bfloat16 [4, 1024], P(None, 'shard'), may hold values from -1.1953125 to 1.1953125
- gate_up: bfloat16 [2, 1024, 2730], P(None, 'shard', 'tp'), may hold values from -0.1875 to 0.1875
- hidden_biases: bfloat16 [3, 2730], P(None, 'tp'), may hold values from -1.1953125 to 1.1953125
- hidden_gain: bfloat16 [2730], P('tp'), may hold values from 0.5 to 1.5
- down_weight: bfloat16 [2730, 1024], P('tp', 'shard'), may hold values from -0.109375 to 0.109375
Outputs:
- output: bfloat16 [16, 1032, 1024], P('shard', 'ctx')
- tokens_grad: float32 [16, 1032, 1024], P('shard', 'ctx')
- qkv_grad: float32 [3, 1024, 1024], P(None, 'shard', 'tp')
- head_biases_grad: float32 [3, 16, 64], P(None, 'tp', 'shard')
- head_gain_grad: float32 [16, 64], P('tp', 'shard')
- out_weight_grad: float32 [1024, 1024], P('tp', 'shard')
- norm_gains_grad: float32 [2, 1024], P(None, 'shard')
- width_biases_grad: float32 [4, 1024], P(None, 'shard')
- gate_up_grad: float32 [2, 1024, 2730], P(None, 'shard', 'tp')
- hidden_biases_grad: float32 [3, 2730], P(None, 'tp')
- hidden_gain_grad: float32 [2730], P('tp')
- down_weight_grad: float32 [2730, 1024], P('tp', 'shard')
Inputs may be any that keep to these rules, and one draw needn't show every extreme that they name: `valid_tokens`: valid slots of each image form a prefix: the class token at slot 0 and 32 * w patch tokens after it, where w is 31 or 32; among the 2 images of each index of shard, one has w = 32. `places`: for a valid slot t >= 1 of an image with w columns the row is (t - 1) // w and the column (t - 1) % w; slot 0 and padding slots hold 0 and 0.
All inputs are finite; a program needn't handle non-finite values.
Results may differ from a plain program's by a relative error of at most 0.02.
Values may be sent and summed in bfloat16 or wider, within the bound.
A program may use at most 256 MiB of HBM per device.

v0:
```python
import functools
import math

import jax
import jax.numpy as jnp
from jax import lax
from jax.experimental import pallas as pl
from jax.experimental.pallas import tpu as pltpu
from jax.sharding import PartitionSpec as P

SHARD, CTX, TP = "shard", "ctx", "tp"


EPS = 1e-06


def standardize(values):
    average = jnp.mean(values, axis=-1, keepdims=True)
    centred = values - average
    spread = lax.rsqrt(jnp.mean(centred * centred, axis=-1, keepdims=True) + EPS)
    return (centred * spread, spread)


def norm_back(grad_hat, normed, spread):
    mean_one = jnp.mean(grad_hat, axis=-1, keepdims=True)
    mean_two = jnp.mean(grad_hat * normed, axis=-1, keepdims=True)
    return (grad_hat - mean_one - normed * mean_two) * spread


def angle_table(row_ids, col_ids, head_size):
    quarter = head_size // 4
    frequency = 10000.0 ** (-jnp.arange(quarter, dtype=jnp.float32) / quarter)
    row_part = row_ids.astype(jnp.float32)[:, None] * frequency[None, :]
    col_part = col_ids.astype(jnp.float32)[:, None] * frequency[None, :]
    return jnp.concatenate([row_part, row_part, col_part, col_part], axis=1)


def turn_half(values):
    quarter = values.shape[-1] // 4
    part_one = values[..., :quarter]
    part_two = values[..., quarter : 2 * quarter]
    part_three = values[..., 2 * quarter : 3 * quarter]
    part_four = values[..., 3 * quarter :]
    return jnp.concatenate([-part_two, part_one, -part_four, part_three], axis=-1)


def rotate(values, angles):
    return values * jnp.cos(angles)[None, :, :] + turn_half(values) * jnp.sin(angles)[None, :, :]


def unrotate(values, angles):
    return values * jnp.cos(angles)[None, :, :] - turn_half(values) * jnp.sin(angles)[None, :, :]


def head_major(values, heads, head_size):
    return values.reshape(values.shape[0], heads, head_size).transpose(1, 0, 2)


def column_sum(values):
    return jnp.sum(values.astype(jnp.float32), axis=0)


def general_plan(
    tokens,
    cotangent,
    valid_tokens,
    places,
    qkv_weight,
    head_biases,
    head_gain,
    out_weight,
    norm_gains,
    width_biases,
    gate_up,
    hidden_biases,
    hidden_gain,
    down_weight,
):
    micro = tokens.shape[0]
    width = tokens.shape[2]
    local_dim = qkv_weight.shape[2]
    local_heads = head_biases.shape[1]
    head_size = local_dim // local_heads
    local_hidden = hidden_gain.shape[0]
    FF = local_hidden * lax.axis_size(TP)
    score_scale = 1.0 / math.sqrt(head_size)
    f32 = jnp.float32
    bf16 = jnp.bfloat16

    def one_batch(batch_idx, carried):
        gathered = (
            lax.all_gather(qkv_weight, SHARD, axis=1, tiled=True),
            lax.all_gather(head_biases, SHARD, axis=2, tiled=True),
            lax.all_gather(head_gain, SHARD, axis=1, tiled=True),
            lax.all_gather(out_weight, SHARD, axis=1, tiled=True),
            lax.all_gather(norm_gains, SHARD, axis=1, tiled=True),
            lax.all_gather(width_biases, SHARD, axis=1, tiled=True),
            lax.all_gather(gate_up, SHARD, axis=1, tiled=True),
            lax.all_gather(down_weight, SHARD, axis=1, tiled=True),
        )
        qkv_full, head_bias, head_scale, out_full, norm_scale, width_bias, gate_full, down_full = (
            gathered
        )
        head_bias_f = head_bias.astype(f32)
        head_scale_f = head_scale.astype(f32)[:, None, :]
        norm_scale = norm_scale.astype(f32)
        width_bias = width_bias.astype(f32)
        hidden_bias = hidden_biases.astype(f32)
        hidden_scale = hidden_gain.astype(f32)
        out_heads = out_full.reshape(local_heads, head_size, width)
        token_rows = lax.dynamic_index_in_dim(tokens, batch_idx, 0, keepdims=False).astype(f32)
        cot_rows = lax.dynamic_index_in_dim(cotangent, batch_idx, 0, keepdims=False).astype(f32)
        valid_row = lax.dynamic_index_in_dim(valid_tokens, batch_idx, 0, keepdims=False) > 0
        row_ids = lax.dynamic_index_in_dim(places[0], batch_idx, 0, keepdims=False)
        col_ids = lax.dynamic_index_in_dim(places[1], batch_idx, 0, keepdims=False)
        angles = angle_table(row_ids, col_ids, head_size)
        normed_one, spread_one = standardize(token_rows)
        first_in = (normed_one * norm_scale[0] + width_bias[0]).astype(bf16)
        query_flat = jnp.dot(first_in, qkv_full[0], preferred_element_type=f32)
        key_flat = jnp.dot(first_in, qkv_full[1], preferred_element_type=f32)
        value_flat = jnp.dot(first_in, qkv_full[2], preferred_element_type=f32)
        query_pre = head_major(query_flat, local_heads, head_size) + head_bias_f[0][:, None, :]
        key_pre = head_major(key_flat, local_heads, head_size)
        value_local = (
            head_major(value_flat, local_heads, head_size) + head_bias_f[1][:, None, :]
        ).astype(bf16)
        queries = rotate(query_pre, angles).astype(bf16)
        key_local = rotate(key_pre, angles).astype(bf16)
        key_heads, value_heads = (
            lax.all_gather(key_local, CTX, axis=1, tiled=True),
            lax.all_gather(value_local, CTX, axis=1, tiled=True),
        )

        def score_block():
            raw = (
                jnp.einsum("htd,hsd->hts", queries, key_heads, preferred_element_type=f32)
                * score_scale
            )
            return jnp.where(valid_row[None, None, :], raw, -1e30)

        scores = score_block()
        row_top = jnp.max(scores, axis=-1, keepdims=True)
        row_total = jnp.sum(jnp.exp(scores - row_top), axis=-1, keepdims=True)
        soft_low = (jnp.exp(scores - row_top) / row_total).astype(bf16)
        mixed = jnp.einsum("hts,hsd->htd", soft_low, value_heads, preferred_element_type=f32)
        mix_sums = lax.psum(
            (
                jnp.sum(mixed, axis=(0, 2), keepdims=True),
                jnp.sum(mixed * mixed, axis=(0, 2), keepdims=True),
            ),
            TP,
        )
        mix_mean = mix_sums[0] / width
        spread_mix = lax.rsqrt(mix_sums[1] / width - mix_mean * mix_mean + EPS)
        mix_hat = (mixed - mix_mean) * spread_mix
        mix_in = (mix_hat * head_scale_f + head_bias_f[2][:, None, :]).astype(bf16)
        branch = lax.psum(
            jnp.einsum("htd,hdn->tn", mix_in, out_heads, preferred_element_type=f32), TP
        )
        resid = token_rows + (branch + width_bias[2])
        normed_two, spread_two = standardize(resid)
        second_in = (normed_two * norm_scale[1] + width_bias[1]).astype(bf16)
        gate_pre = jnp.dot(second_in, gate_full[0], preferred_element_type=f32) + hidden_bias[0]
        up_pre = jnp.dot(second_in, gate_full[1], preferred_element_type=f32) + hidden_bias[1]
        sigmoid_gate = jax.nn.sigmoid(gate_pre)
        silu_gate = gate_pre * sigmoid_gate
        hidden = silu_gate * up_pre
        hidden_sums = lax.psum(
            (
                jnp.sum(hidden, axis=-1, keepdims=True),
                jnp.sum(hidden * hidden, axis=-1, keepdims=True),
            ),
            TP,
        )
        hidden_mean = hidden_sums[0] / FF
        spread_hid = lax.rsqrt(hidden_sums[1] / FF - hidden_mean * hidden_mean + EPS)
        hidden_hat = (hidden - hidden_mean) * spread_hid
        down_in = (hidden_hat * hidden_scale + hidden_bias[2]).astype(bf16)
        ffn_out = lax.psum(
            jnp.dot(down_in, down_full, preferred_element_type=f32).astype(jnp.bfloat16), TP
        ).astype(jnp.float32)
        result = (resid + (ffn_out + width_bias[3])).astype(bf16)
        d_ffn_low = cot_rows.astype(bf16)
        g_down = jnp.einsum("tf,td->fd", down_in, d_ffn_low, preferred_element_type=f32)
        d_down_in = jnp.einsum("td,fd->tf", d_ffn_low, down_full, preferred_element_type=f32)
        grad_hid = d_down_in * hidden_scale
        hid_back = lax.psum(
            (
                jnp.sum(grad_hid, axis=-1, keepdims=True),
                jnp.sum(grad_hid * hidden_hat, axis=-1, keepdims=True),
            ),
            TP,
        )
        d_hidden = (grad_hid - hid_back[0] / FF - hidden_hat * (hid_back[1] / FF)) * spread_hid
        d_gate = (
            d_hidden * up_pre * sigmoid_gate * (1.0 + gate_pre * (1.0 - sigmoid_gate))
        ).astype(bf16)
        d_up = (d_hidden * silu_gate).astype(bf16)
        g_gate_one = jnp.einsum("td,tf->df", second_in, d_gate, preferred_element_type=f32)
        g_up_one = jnp.einsum("td,tf->df", second_in, d_up, preferred_element_type=f32)
        d_second_part = jnp.einsum(
            "tf,df->td", d_gate, gate_full[0], preferred_element_type=f32
        ) + jnp.einsum("tf,df->td", d_up, gate_full[1], preferred_element_type=f32)
        d_second = lax.psum(d_second_part, TP)
        d_resid = cot_rows + norm_back(d_second * norm_scale[1], normed_two, spread_two)
        d_branch_low = d_resid.astype(bf16)
        g_out = jnp.einsum("htd,tn->hdn", mix_in, d_branch_low, preferred_element_type=f32).reshape(
            local_dim, width
        )
        d_mix_in = jnp.einsum("tn,hdn->htd", d_branch_low, out_heads, preferred_element_type=f32)
        grad_mix = d_mix_in * head_scale_f
        mix_back = lax.psum(
            (
                jnp.sum(grad_mix, axis=(0, 2), keepdims=True),
                jnp.sum(grad_mix * mix_hat, axis=(0, 2), keepdims=True),
            ),
            TP,
        )
        d_mixed = (
            (grad_mix - mix_back[0] / width - mix_hat * (mix_back[1] / width)) * spread_mix
        ).astype(bf16)
        again = score_block()
        weights_soft = jnp.exp(again - row_top) / row_total
        d_soft = jnp.einsum("htd,hsd->hts", d_mixed, value_heads, preferred_element_type=f32)
        row_dot = jnp.sum(weights_soft * d_soft, axis=-1, keepdims=True)
        d_scores = (weights_soft * (d_soft - row_dot)).astype(bf16)
        d_query = (
            jnp.einsum("hts,hsd->htd", d_scores, key_heads, preferred_element_type=f32)
            * score_scale
        )
        soft_again = weights_soft.astype(bf16)
        d_key_all = (
            jnp.einsum("hts,htd->hsd", d_scores, queries, preferred_element_type=f32) * score_scale
        )
        d_value_all = jnp.einsum("hts,htd->hsd", soft_again, d_mixed, preferred_element_type=f32)
        d_key_heads, d_value_loc = (
            lax.psum_scatter(
                d_key_all.astype(jnp.bfloat16), CTX, scatter_dimension=1, tiled=True
            ).astype(jnp.float32),
            lax.psum_scatter(
                d_value_all.astype(jnp.bfloat16), CTX, scatter_dimension=1, tiled=True
            ).astype(jnp.float32),
        )
        d_query_low = unrotate(d_query, angles).astype(bf16)
        d_key_low = unrotate(d_key_heads, angles).astype(bf16)
        d_value_low = d_value_loc.astype(bf16)
        g_query = jnp.einsum(
            "tn,htd->nhd", first_in, d_query_low, preferred_element_type=f32
        ).reshape(width, local_dim)
        g_key = jnp.einsum("tn,htd->nhd", first_in, d_key_low, preferred_element_type=f32).reshape(
            width, local_dim
        )
        g_value = jnp.einsum(
            "tn,htd->nhd", first_in, d_value_low, preferred_element_type=f32
        ).reshape(width, local_dim)
        d_first_part = jnp.einsum(
            "htd,nhd->tn",
            d_query_low,
            qkv_full[0].reshape(width, local_heads, head_size),
            preferred_element_type=f32,
        )
        d_first_part = d_first_part + jnp.einsum(
            "htd,nhd->tn",
            d_key_low,
            qkv_full[1].reshape(width, local_heads, head_size),
            preferred_element_type=f32,
        )
        d_first_part = d_first_part + jnp.einsum(
            "htd,nhd->tn",
            d_value_low,
            qkv_full[2].reshape(width, local_heads, head_size),
            preferred_element_type=f32,
        )
        d_first = lax.psum(d_first_part.astype(jnp.bfloat16), TP).astype(jnp.float32)
        d_tokens = d_resid + norm_back(d_first * norm_scale[0], normed_one, spread_one)
        g_head_bias = jnp.stack(
            [
                jnp.sum(d_query_low.astype(f32), axis=1),
                jnp.sum(d_value_low.astype(f32), axis=1),
                jnp.sum(d_mix_in, axis=1),
            ]
        )
        g_head_scale = jnp.sum(d_mix_in * mix_hat, axis=1)
        g_norm = jnp.stack([column_sum(d_first * normed_one), column_sum(d_second * normed_two)])
        g_width = jnp.stack(
            [
                column_sum(d_first),
                column_sum(d_second),
                column_sum(d_branch_low),
                column_sum(d_ffn_low),
            ]
        )
        g_hidden_bias = jnp.stack([column_sum(d_gate), column_sum(d_up), column_sum(d_down_in)])
        g_hidden_scale = column_sum(d_down_in * hidden_hat)
        out_all = lax.dynamic_update_index_in_dim(carried[0], result, batch_idx, 0)
        grad_all = lax.dynamic_update_index_in_dim(carried[1], d_tokens, batch_idx, 0)
        updates = (
            g_query,
            g_key,
            g_value,
            g_head_bias,
            g_head_scale,
            g_out,
            g_norm,
            g_width,
            g_gate_one,
            g_up_one,
            g_down,
            g_hidden_bias,
            g_hidden_scale,
        )
        return (
            out_all,
            grad_all,
            tuple((before + added for before, added in zip(carried[2], updates))),
        )

    zeros_acc = (
        jnp.zeros((width, local_dim), f32),
        jnp.zeros((width, local_dim), f32),
        jnp.zeros((width, local_dim), f32),
        jnp.zeros((3, local_heads, head_size), f32),
        jnp.zeros((local_heads, head_size), f32),
        jnp.zeros((local_dim, width), f32),
        jnp.zeros((2, width), f32),
        jnp.zeros((4, width), f32),
        jnp.zeros((width, local_hidden), f32),
        jnp.zeros((width, local_hidden), f32),
        jnp.zeros((local_hidden, width), f32),
        jnp.zeros((3, local_hidden), f32),
        jnp.zeros((local_hidden,), f32),
    )
    start = (jnp.zeros(tokens.shape, bf16), jnp.zeros(tokens.shape, f32), zeros_acc)
    out_all, grad_all, summed = lax.fori_loop(0, micro, one_batch, start)
    (
        acc_query,
        acc_key,
        acc_value,
        acc_head_bias,
        acc_head_scale,
        acc_out,
        acc_norm,
        acc_width,
        acc_gate_one,
        acc_up_one,
        acc_down,
        acc_hidden_bias,
        acc_hidden_scale,
    ) = summed
    acc_qkv = jnp.stack([acc_query, acc_key, acc_value])
    acc_gate = jnp.stack([acc_gate_one, acc_up_one])
    sharded = (
        acc_qkv,
        acc_head_bias,
        acc_head_scale,
        acc_out,
        acc_norm,
        acc_width,
        acc_gate,
        acc_down,
    )
    hidden_done = lax.psum((acc_hidden_bias, acc_hidden_scale), (SHARD, CTX))
    return (
        out_all,
        grad_all,
        lax.psum_scatter(
            lax.psum(sharded[0].astype(jnp.bfloat16), CTX),
            SHARD,
            scatter_dimension=1,
            tiled=True,
        ).astype(jnp.float32),
        lax.psum_scatter(
            lax.psum(sharded[1].astype(jnp.bfloat16), CTX),
            SHARD,
            scatter_dimension=2,
            tiled=True,
        ).astype(jnp.float32),
        lax.psum_scatter(
            lax.psum(sharded[2].astype(jnp.bfloat16), CTX),
            SHARD,
            scatter_dimension=1,
            tiled=True,
        ).astype(jnp.float32),
        lax.psum_scatter(
            lax.psum(sharded[3].astype(jnp.bfloat16), CTX),
            SHARD,
            scatter_dimension=1,
            tiled=True,
        ).astype(jnp.float32),
        lax.psum_scatter(
            lax.psum(sharded[4].astype(jnp.bfloat16), CTX),
            SHARD,
            scatter_dimension=1,
            tiled=True,
        ).astype(jnp.float32),
        lax.psum_scatter(
            lax.psum(sharded[5].astype(jnp.bfloat16), CTX),
            SHARD,
            scatter_dimension=1,
            tiled=True,
        ).astype(jnp.float32),
        lax.psum_scatter(
            lax.psum(sharded[6].astype(jnp.bfloat16), CTX),
            SHARD,
            scatter_dimension=1,
            tiled=True,
        ).astype(jnp.float32),
        hidden_done[0],
        hidden_done[1],
        lax.psum_scatter(
            lax.psum(sharded[7].astype(jnp.bfloat16), CTX),
            SHARD,
            scatter_dimension=1,
            tiled=True,
        ).astype(jnp.float32),
    )


MESH = pl.DeviceIdType.MESH
LIMIT = 56 * 1024 * 1024
ANY = pl.BlockSpec(memory_space=pl.ANY)
IN_VMEM = pl.BlockSpec(memory_space=pltpu.VMEM)
CORE, ACROSS, BESIDE, UP, DOWN, SWAP, FAR = range(7)
ROW, COL = range(2)


def place_of():
    index = lax.axis_index(SHARD)
    return (lax.div(index, 2), lax.rem(index, 2), lax.axis_index(CTX), lax.axis_index(TP))


def when(condition, action):
    if condition is None:
        action()
    else:
        pl.when(condition)(action)


def both(first, second):
    return jnp.logical_and(first, second)


def device(place, way):
    z, k, x, y = place
    return {
        CORE: {SHARD: 2 * z + 1 - k},
        ACROSS: {CTX: 1 - x},
        BESIDE: {TP: 1 - y},
        UP: {SHARD: 2 * z + 2 + k},
        DOWN: {SHARD: 2 * z - 2 + k},
        SWAP: {SHARD: 2 * z + 1 - k, CTX: 1 - x},
        FAR: {SHARD: 2 * z + 1 - k, CTX: 1 - x, TP: 1 - y},
    }[way]


def greet(layers, place, diagonals):
    z, k, x, y = place
    barrier = pltpu.get_barrier_semaphore()

    def hello(way):
        pl.semaphore_signal(barrier, inc=1, device_id=device(place, way), device_id_type=MESH)

    hello(CORE)
    hello(ACROSS)
    hello(BESIDE)
    pl.when(z > 0)(lambda: hello(DOWN))
    pl.when(z < layers - 1)(lambda: hello(UP))
    count = 3 + jnp.where(z > 0, 1, 0) + jnp.where(z < layers - 1, 1, 0)
    for way in diagonals:
        pl.when(k != x)(lambda way=way: hello(way))
        count = count + jnp.where(k != x, 1, 0)
    pl.semaphore_wait(barrier, count)


class Links:
    def __init__(self, place, send_sem, recv_sem):
        self.place, self.send_sem, self.recv_sem = place, send_sem, recv_sem
        self.used = 0
        self.sent = []
        self.noted = None

    def take(self, count):
        first = self.used
        self.used += count
        return first

    def copy(self, way, at, source, target):
        return pltpu.make_async_remote_copy(
            src_ref=source,
            dst_ref=target,
            send_sem=self.send_sem.at[at],
            recv_sem=self.recv_sem.at[at],
            device_id=device(self.place, way),
            device_id_type=MESH,
        )

    def do(self, condition, action):
        if self.noted is None:
            when(condition, action)
        else:
            self.noted.append((condition, action))

    def record(self, actions):
        self.noted = []
        for action in actions:
            action()
        found, self.noted = self.noted, None
        return found

    def send(self, condition, copy):
        self.do(condition, copy.start)
        self.sent.append((condition, copy))

    def finish(self):
        for condition, copy in self.sent:
            when(condition, copy.wait_send)


def run(noted):
    for condition, action in noted:
        when(condition, action)


def piece_view(kind, rows, cols, ref, y, s, first, size):
    if kind == ROW:
        at_row, at_col = s * rows + first, y * cols
    else:
        at_row, at_col = y * rows + first, s * cols
    at_row, at_col = pl.multiple_of(at_row, 16), pl.multiple_of(at_col, 128)
    return ref.at[pl.ds(at_row, size), pl.ds(at_col, cols)]


def cut_rows(ref, first, size):
    return ref.at[pl.ds(pl.multiple_of(first, 16), size), :]


class Gather:
    def __init__(self, layers, links, kind, own, full, low, rows, split, local_sem):
        self.layers, self.links, self.kind, self.own, self.full = layers, links, kind, own, full
        self.piece_rows, self.cols = own.shape
        self.low, self.rows = low, rows
        self.split, self.half = split, split // 2
        self.local_sem = local_sem
        n = layers
        self.z_a = links.take(2 * n)
        self.z_b = links.take(2 * n)
        self.x_a, self.x_b = links.take(n), links.take(n)
        self.y_a, self.y_b = links.take(n), links.take(1)
        self.core = links.take(2 * n)

    @staticmethod
    def sem_count(layers):
        return 9 * layers + 1

    def copy(self, way, at, y, z, first, size, from_own=False, other_core=False):
        k = self.links.place[1]
        s = 2 * z + (1 - k if other_core else k)
        first = first + self.low
        there = piece_view(self.kind, self.piece_rows, self.cols, self.full, y, s, first, size)
        here = cut_rows(self.own, first, size) if from_own else there
        return self.links.copy(way, at, here, there)

    def half_a(self, way, at, y, z, which, from_own=False):
        return self.copy(way, at, y, z, which * self.half, self.half, from_own)

    def part_a(self, way, at, y, z, from_own=False):
        return self.copy(way, at, y, z, 0, self.split, from_own)

    def part_b(self, way, at, y, z, from_own=False):
        return self.copy(way, at, y, z, self.split, self.rows - self.split, from_own)

    def to_core(self, y, z, from_own=False, other_core=False):
        return self.copy(CORE, self.core + 2 * z + y, y, z, 0, self.rows, from_own, other_core)

    def z_at(self, base, way, z):
        return base + (0 if way == UP else self.layers) + z

    def begin(self):
        z, k, x, y = self.links.place
        send = self.links.send
        low, high = z > 0, z < self.layers - 1
        own_view = piece_view(
            self.kind, self.piece_rows, self.cols, self.full, y, 2 * z + k, self.low, self.rows
        )
        own = cut_rows(self.own, self.low, self.rows)
        self.local = pltpu.make_async_copy(own, own_view, self.local_sem)
        if self.split < self.rows:
            send(None, self.part_b(BESIDE, self.y_b, y, z, True))
            same = x == y
            send(both(same, high), self.part_b(UP, self.z_at(self.z_b, UP, z), y, z, True))
            send(both(same, low), self.part_b(DOWN, self.z_at(self.z_b, DOWN, z), y, z, True))
        if self.split:
            send(high, self.half_a(UP, self.z_at(self.z_a, UP, z), y, z, x, True))
            send(low, self.half_a(DOWN, self.z_at(self.z_a, DOWN, z), y, z, x, True))
            send(None, self.part_a(BESIDE, self.y_a + z, y, z, True))
        send(None, self.to_core(y, z, True))
        self.links.do(None, self.local.start)

    def cross_y(self):
        if self.split == self.rows:
            return
        z, k, x, y = self.links.place
        send = self.links.send
        self.links.do(None, self.part_b(BESIDE, self.y_b, 1 - y, z).wait_recv)
        other = x != y
        low, high = z > 0, z < self.layers - 1
        send(both(other, high), self.part_b(UP, self.z_at(self.z_b, UP, z), 1 - y, z))
        send(both(other, low), self.part_b(DOWN, self.z_at(self.z_b, DOWN, z), 1 - y, z))

    def steps(self, step):
        z = self.links.place[0]
        below, above = z - 1 - step, z + 1 + step
        return (
            (UP, below, below >= 0, z < self.layers - 1),
            (DOWN, above, above <= self.layers - 1, z > 0),
        )

    def along_z(self, step):
        z, k, x, y = self.links.place
        send = self.links.send
        for way, origin, there, further in self.steps(step):
            if self.split < self.rows:
                came = self.part_b(way, self.z_at(self.z_b, way, origin), x, origin)
                self.links.do(there, came.wait_recv)
                send(both(there, further), came)
                send(there, self.part_b(ACROSS, self.x_b + origin, x, origin))
            if self.split:
                came = self.half_a(way, self.z_at(self.z_a, way, origin), y, origin, x)
                self.links.do(there, came.wait_recv)
                send(both(there, further), came)
                send(there, self.half_a(ACROSS, self.x_a + origin, y, origin, x))

    def along_x(self, step):
        z, k, x, y = self.links.place
        send = self.links.send
        for way, origin, there, further in self.steps(step):
            if self.split:
                self.links.do(there, self.half_a(ACROSS, self.x_a + origin, y, origin, 1 - x).wait_recv)
                send(there, self.part_a(BESIDE, self.y_a + origin, y, origin))
            if self.split < self.rows:
                self.links.do(there, self.part_b(ACROSS, self.x_b + origin, 1 - x, origin).wait_recv)
            send(there, self.to_core(y, origin))

    def along_y(self, step):
        z, k, x, y = self.links.place
        todo = ((None, z, None, None),) if step < 0 else self.steps(step)
        for way, origin, there, further in todo:
            if self.split:
                self.links.do(there, self.part_a(BESIDE, self.y_a + origin, 1 - y, origin).wait_recv)
            self.links.send(there, self.to_core(1 - y, origin))

    def stages(self):
        found = [[self.begin], [self.cross_y]]
        for step in range(self.layers + 1):
            now = []
            if step < self.layers - 1:
                now.append(functools.partial(self.along_z, step))
            if step == 0:
                now.append(functools.partial(self.along_y, -1))
            if 0 <= step - 1 < self.layers - 1:
                now.append(functools.partial(self.along_x, step - 1))
            if 0 <= step - 2 < self.layers - 1:
                now.append(functools.partial(self.along_y, step - 2))
            found.append(now)
        return found

    def arrived(self):
        self.links.do(None, self.local.wait)
        for layer in range(self.layers):
            for y in range(2):
                self.links.do(None, self.to_core(y, layer, other_core=True).wait_recv)


def ticks_of(links, jobs, starts, begins):
    plans = [job.stages() for job in jobs]
    ticks = [[] for _ in range(max([at + len(plan) for at, plan in zip(starts, plans)]))]
    for start, begin, plan in zip(starts, begins, plans):
        for stage, actions in enumerate(plan):
            ticks[start + stage if stage else begin] += actions
    return [links.record(tick) for tick in ticks]


class Swap:
    def __init__(self, links, source, target, local_sem):
        z, k, x, y = links.place
        self.same, self.other = k == x, k != x
        self.here = pltpu.make_async_copy(source, target, local_sem)
        self.there = links.copy(SWAP, links.take(1), source, target)

    def begin(self):
        pl.when(self.same)(self.here.start)
        pl.when(self.other)(self.there.start)

    def arrived(self):
        pl.when(self.same)(self.here.wait)
        pl.when(self.other)(self.there.wait)


class Cross:
    def __init__(self, links, source, target, local_sem):
        y = links.place[3]
        at = links.take(1)
        self.here = pltpu.make_async_copy(source, target.at[y], local_sem)
        self.out = links.copy(BESIDE, at, source, target.at[y])
        self.back = links.copy(BESIDE, at, source, target.at[1 - y])

    def begin(self):
        self.here.start()
        self.out.start()

    def arrived(self):
        self.here.wait()
        self.out.wait_send()
        self.back.wait_recv()


class Spread:
    def __init__(self, links, block, both_images, local_sem):
        z, k, x, y = links.place
        self.same, self.other = k == x, k != x
        here, first, second = links.take(1), links.take(1), 0
        target = both_images.at[y]
        self.keep = pltpu.make_async_copy(block, target, local_sem)
        self.beside = links.copy(BESIDE, here, block, target)
        self.swap = links.copy(SWAP, first, block, target)
        self.far = links.copy(FAR, here, block, target)
        self.came = links.copy(BESIDE, here, block, both_images.at[1 - y])

    def begin(self):
        def same():
            self.keep.start()
            self.beside.start()

        def other():
            self.swap.start()
            self.far.start()

        pl.when(self.same)(same)
        pl.when(self.other)(other)

    def arrived(self):
        def same():
            self.keep.wait()
            self.beside.wait_send()

        def other():
            self.swap.wait()
            self.far.wait_send()

        pl.when(self.same)(same)
        pl.when(self.other)(other)
        self.came.wait_recv()


def full_shape(layers, kind, piece):
    if kind == ROW:
        return piece[:-2] + (piece[-2] * layers * 2, piece[-1] * 2)
    return (piece[-2] * 2, piece[-1] * layers * 2)


def by_chunks(shape, body):
    rows, cols = shape
    chunk = 16
    while rows % (2 * chunk) == 0 and 2 * chunk * cols <= 16384:
        chunk *= 2

    def step(i, nothing):
        body((pl.ds(pl.multiple_of(i * chunk, 16), chunk), slice(None)))
        return nothing

    lax.fori_loop(0, rows // chunk, step, 0)


def add_into(target, term):
    def body(where):
        target[where] = target[where] + term[where]

    by_chunks(target.shape, body)


def store_sum(out, *terms):
    def body(where):
        total = terms[0][where].astype(jnp.float32)
        for term in terms[1:]:
            total = total + term[where].astype(jnp.float32)
        out[where] = total

    by_chunks(out.shape, body)


class Reduce:
    def __init__(self, layers, links, kind, grad, out, low, split, scratch, local_sem, local_base):
        self.layers, self.links, self.kind, self.grad = layers, links, kind, grad
        self.mine, self.load, self.y_in, self.x_in, self.z_in, self.last = scratch
        self.sent = []
        self.rows, self.cols = self.mine.shape[-2:]
        self.low, self.piece_rows = low, out.shape[0]
        self.out = cut_rows(out, low, self.rows)
        self.split = split
        self.local_sem, self.local_base = local_sem, local_base
        n = layers
        self.core = links.take(2 * n)
        self.y_a, self.x_b = links.take(n), links.take(n)
        self.z_a, self.z_b = links.take(2 * n), links.take(2 * n)
        self.end_a, self.end_b, self.end_c = links.take(1), links.take(1), links.take(1)
        self.order = []
        low, high = 0, layers - 1
        while low <= high:
            self.order.append(high)
            if low < high:
                self.order.append(low)
            low, high = low + 1, high - 1

    @staticmethod
    def sem_count(layers):
        return 8 * layers + 3

    def part_a(self, ref):
        return cut_rows(ref, 0, self.split)

    def part_b(self, ref):
        return cut_rows(ref, self.split, self.rows - self.split)

    def send(self, condition, copy):
        self.links.do(condition, copy.start)
        self.sent.append((condition, copy))

    def finish(self):
        for condition, copy in self.sent:
            when(condition, copy.wait_send)

    def add(self, condition, target, term):
        self.links.do(condition, functools.partial(add_into, target, term))

    def grad_piece(self, y, s):
        return piece_view(
            self.kind, self.piece_rows, self.cols, self.grad, y, s, self.low, self.rows
        )

    def local(self, number):
        k = self.links.place[1]
        layer, y = self.order[number // 2], number % 2
        return pltpu.make_async_copy(
            self.grad_piece(y, 2 * layer + k),
            self.load.at[number % 2],
            self.local_sem.at[self.local_base + number],
        )

    def to_core(self, y, layer):
        k = self.links.place[1]
        return self.links.copy(
            CORE,
            self.core + 2 * layer + y,
            self.grad_piece(y, 2 * layer + 1 - k),
            self.mine.at[y, layer],
        )

    def begin(self):
        for layer in self.order:
            for y in range(2):
                self.send(None, self.to_core(y, layer))
        for number in range(2):
            self.links.do(None, self.local(number).start)

    def to_y(self, layer):
        y = self.links.place[3]
        source = self.part_a(self.mine.at[1 - y, layer])
        return self.links.copy(BESIDE, self.y_a + layer, source, self.y_in.at[layer])

    def to_x(self, layer):
        x = self.links.place[2]
        source = self.part_b(self.mine.at[1 - x, layer])
        return self.links.copy(ACROSS, self.x_b + layer, source, self.x_in.at[layer])

    def chip_sum(self):
        for number in range(2 * self.layers):
            layer, side = self.order[number // 2], number % 2
            self.links.do(None, self.local(number).wait)
            self.links.do(None, self.to_core(side, layer).wait_recv)
            self.add(None, self.mine.at[side, layer], self.load.at[number % 2])
            if number + 2 < 2 * self.layers:
                self.links.do(None, self.local(number + 2).start)
            if side:
                self.send(None, self.to_y(layer))
                self.send(None, self.to_x(layer))

    def plane_sum(self):
        z, k, x, y = self.links.place
        for layer in self.order:
            self.links.do(None, self.to_y(layer).wait_recv)
            self.add(None, self.part_a(self.mine.at[y, layer]), self.y_in.at[layer])
            self.links.do(None, self.to_x(layer).wait_recv)
            self.add(None, self.part_b(self.mine.at[x, layer]), self.x_in.at[layer])

    def chain(self, way, layer, receiver):
        z, k, x, y = self.links.place
        slot = layer if way == UP else jnp.where(receiver == layer, self.layers, layer)
        add = 0 if way == UP else self.layers
        found = []
        for base, part, side in ((self.z_a, self.part_a, y), (self.z_b, self.part_b, x)):
            total, box = part(self.mine.at[side, layer]), part(self.z_in.at[slot])
            found.append((total, box, self.links.copy(way, base + add + layer, total, box)))
        return found

    def take(self, condition, way, layer):
        for total, box, copy in self.chain(way, layer, self.links.place[0]):
            self.links.do(condition, copy.wait_recv)
            self.add(condition, total, box)

    def along_z(self, depth):
        z = self.links.place[0]
        top = self.layers - 1
        for way, here, goals in (
            (UP, z == depth, range(top, depth, -1)),
            (DOWN, z == top - depth, range(0, top - depth)),
        ):
            for layer in goals:
                if depth:
                    self.take(here, way, layer)
                for total, box, copy in self.chain(way, layer, z + 1 if way == UP else z - 1):
                    self.send(here, copy)

    def ending(self):
        z, k, x, y = self.links.place
        self.take(z > 0, UP, z)
        self.take(z < self.layers - 1, DOWN, z)
        self.sum_a, self.sum_b = self.part_a(self.mine.at[y, z]), self.part_b(self.mine.at[x, z])
        self.got_a, self.got_b = self.part_a(self.last.at[0]), self.part_b(self.last.at[0])
        self.got_y = self.part_b(self.last.at[1])
        self.x_end = self.links.copy(ACROSS, self.end_a, self.sum_a, self.got_a)
        self.y_end = self.links.copy(BESIDE, self.end_b, self.sum_b, self.got_y)
        self.x_last = self.links.copy(ACROSS, self.end_c, self.sum_b, self.got_b)
        self.send(y != x, self.y_end)
        self.send(None, self.x_end)

    def owner(self):
        z, k, x, y = self.links.place

        self.links.do(y == x, self.y_end.wait_recv)
        self.add(y == x, self.sum_b, self.got_y)
        self.send(y == x, self.x_last)
        self.links.do(None, self.x_end.wait_recv)
        out_a = self.part_a(self.out)
        self.links.do(None, functools.partial(store_sum, out_a, self.sum_a, self.got_a))

    def write(self):
        z, k, x, y = self.links.place
        out_b = self.part_b(self.out)

        self.links.do(y != x, self.x_last.wait_recv)
        self.links.do(y != x, functools.partial(store_sum, out_b, self.got_b))
        self.links.do(y == x, functools.partial(store_sum, out_b, self.sum_b))

    def stages(self):
        chains = [[functools.partial(self.along_z, depth)] for depth in range(self.layers - 1)]
        return [
            [self.begin], [self.chip_sum], [self.plane_sum], *chains,
            [self.ending], [self.owner], [self.write],
        ]


class Total:
    def __init__(self, layers, links, given, out, boxes, layer_boxes):
        self.layers, self.links, self.given, self.out = layers, links, given, out
        self.boxes, self.layer_boxes = boxes, layer_boxes
        self.pair = [links.take(1) for _ in range(3)]
        self.z_up, self.z_down = links.take(layers), links.take(layers)

    @staticmethod
    def sem_count(layers):
        return 3 + 2 * layers

    def exchange(self, number):
        way = (CORE, ACROSS, BESIDE)[number]
        source = self.given if number == 0 else self.boxes.at[2 + number]
        return self.links.copy(way, self.pair[number], source, self.boxes.at[number])

    def begin(self):
        self.links.send(None, self.exchange(0))

    def join(self, number):
        z = self.links.place[0]
        self.links.do(None, self.exchange(number).wait_recv)
        mine = self.given if number == 0 else self.boxes.at[2 + number]
        result = self.layer_boxes.at[z] if number == 2 else self.boxes.at[3 + number]
        self.links.do(None, functools.partial(store_sum, result, mine, self.boxes.at[number]))
        if number < 2:
            self.links.send(None, self.exchange(number + 1))
        else:
            self.links.send(z < self.layers - 1, self.pass_on(UP, z))
            self.links.send(z > 0, self.pass_on(DOWN, z))

    def pass_on(self, way, layer):
        box = self.layer_boxes.at[layer]
        return self.links.copy(way, (self.z_up if way == UP else self.z_down) + layer, box, box)

    def along_z(self, step):
        z = self.links.place[0]
        top = self.layers - 1
        below, above = z - 1 - step, z + 1 + step
        for way, origin, there, further in (
            (UP, below, below >= 0, z < top),
            (DOWN, above, above <= top, z > 0),
        ):
            copy = self.pass_on(way, origin)
            self.links.do(there, copy.wait_recv)
            self.links.send(both(there, further), copy)

    def write(self):
        layers = [self.layer_boxes.at[layer] for layer in range(self.layers)]
        self.links.do(None, functools.partial(store_sum, self.out, *layers))

    def stages(self):
        joins = [[functools.partial(self.join, number)] for number in range(3)]
        moves = [[functools.partial(self.along_z, step)] for step in range(self.layers - 1)]
        return [[self.begin], *joins, *moves, [self.write]]


def reduce_jobs(layers, links, jobs, grads, outs, scratch, local_sem):
    todo = []
    for number, (mat, kind, low, rows, split) in enumerate(jobs):
        own = scratch[6 * number : 6 * number + 6]
        at = number * 2 * layers
        grad, out = grads[mat], outs[mat]
        todo.append(Reduce(layers, links, kind, grad, out, low, split, own, local_sem, at))
    return todo


def reduce_shapes(layers, rows, cols, split):
    return [
        (2, layers, rows, cols), (2, rows, cols), (layers, split, cols),
        (layers, rows - split, cols), (layers + 1, rows, cols), (2, rows, cols),
    ]


def piece_shape(layers, kind, full):
    if kind == ROW:
        return full[:-2] + (full[-2] // (2 * layers), full[-1] // 2)
    return (full[-2] // 2, full[-1] // (2 * layers))


def pair_lanes(shape, head_size):
    lane = lax.broadcasted_iota(jnp.int32, shape, len(shape) - 1)
    return lane < head_size


def dot_last(left, right):
    return lax.dot_general(left, right, (((1,), (1,)), ((), ())), preferred_element_type=jnp.float32)


def dot_first(left, right):
    return lax.dot_general(left, right, (((0,), (0,)), ((), ())), preferred_element_type=jnp.float32)


def dot(left, right):
    return lax.dot_general(left, right, (((1,), (0,)), ((), ())), preferred_element_type=jnp.float32)


def only_head(values, head, head_size):
    lane = lax.broadcasted_iota(jnp.int32, (1, values.shape[1]), 1)
    keep = (lane < head_size) if head == 0 else (lane >= head_size)
    return values * jnp.where(keep, 1.0, 0.0).astype(values.dtype)


LOG2_E = 1.4426950408889634


def turn_lanes(values, quarter):
    width = values.shape[-1]
    lane = lax.broadcasted_iota(jnp.int32, (1, width), 1)
    even = lax.rem(lax.div(lane, quarter), 2) == 0
    after = pltpu.roll(values, width - quarter, 1)
    before = pltpu.roll(values, quarter, 1)
    return jnp.where(even, -after, before)


def slot_bias(shape, axis, rows, tokens_here, count):
    slot = lax.broadcasted_iota(jnp.int32, shape, axis)
    second = slot >= rows
    within = jnp.where(second, slot - rows, slot)
    token = jnp.where(second, within + tokens_here, within).astype(jnp.float32)
    return jnp.where(jnp.logical_and(within < tokens_here, token < count), 0.0, -1e30)


def front_kernel(layers, head_size, grid_side, *refs):
    (
        vec_own, qkv_own, out_own, gate_own, down_own, tokens, cot, valid, hidden_own,
        vec_full, qkv_full, out_full, gate_full, down_full, hidden_full, cot_out,
        x_out, n_out, q_out, k_out, v_out, o_out, stat_out, vec_out, count_out, cos, sin,
        x, valid_both, vec, weight, hat, normed, q, keys, values, bias,
        send_sem, recv_sem, local_sem,
    ) = refs
    f32, bf16 = jnp.float32, jnp.bfloat16
    place = place_of()
    z, k, me_x, y = place
    greet(layers, place, (SWAP,))
    links = Links(place, send_sem, recv_sem)
    rows, width = x.shape
    tokens_here = valid.shape[1] // 2
    tile = weight.shape[2]
    quarter = head_size // 4
    lanes = 2 * head_size
    locals_used = [0]

    def local_at():
        locals_used[0] += 1
        return local_sem.at[locals_used[0] - 1]

    block = Swap(links, tokens.at[y], x, local_at())
    cot_block = Swap(links, cot.at[y], cot_out, local_at())
    valid_swap = Swap(links, valid, valid_both, local_at())
    cross = Cross(links, hidden_own, hidden_full, local_at())
    out_rows, down_rows = out_own.shape[0], down_own.shape[0] // 2
    todo = [
        (ROW, vec_own, vec_full, 0, vec_own.shape[0], 0),
        (ROW, qkv_own.at[0], qkv_full.at[0], 0, 128, 64),
        (ROW, qkv_own.at[1], qkv_full.at[1], 0, 128, 64),
        (ROW, qkv_own.at[2], qkv_full.at[2], 0, 128, 64),
        (ROW, gate_own.at[0], gate_full.at[0], 0, 64, 32),
        (ROW, gate_own.at[0], gate_full.at[0], 64, 64, 32),
        (ROW, gate_own.at[1], gate_full.at[1], 0, 64, 32),
        (ROW, gate_own.at[1], gate_full.at[1], 64, 64, 32),
        (COL, down_own, down_full, 0, down_rows, 448),
        (COL, down_own, down_full, down_rows, down_rows, 448),
        (COL, out_own, out_full, 0, out_rows, 320),
    ]
    starts = (0, 1, 2, 3, 4, 5, 6, 7, 8, 9, 10)
    begins = (0, 0, 1, 2, 3, 4, 5, 6, 7, 8, 9)
    jobs = [
        Gather(layers, links, kind, own, full, low, size, split, local_at())
        for kind, own, full, low, size, split in todo
    ]
    ticks = ticks_of(links, jobs, starts, begins)
    weight_loads = []
    for mat in range(3):
        for part in range(width // tile):
            slot = len(weight_loads) % 2
            weight_loads.append(
                pltpu.make_async_copy(
                    qkv_full.at[mat, :, pl.ds(part * tile, tile)], weight.at[slot], local_at()
                )
            )
    vec_load = pltpu.make_async_copy(vec_full, vec, local_at())
    keeps = [
        pltpu.make_async_copy(source, target, local_at())
        for source, target in ((x, x_out), (normed, n_out), (q, q_out), (keys, k_out), (values, v_out))
    ]
    shares = []
    my_rows = pl.ds(pl.multiple_of(k * rows, 16), rows)
    other_rows = pl.ds(pl.multiple_of((1 - k) * rows, 16), rows)
    for store in (keys, values):
        for part in range(width // tile):
            at = links.take(1)
            cols = pl.ds(part * tile, tile)
            out_going = links.copy(CORE, at, store.at[my_rows, cols], store.at[my_rows, cols])
            coming = links.copy(CORE, at, store.at[other_rows, cols], store.at[other_rows, cols])
            shares.append((out_going, coming))

    block.begin()
    valid_swap.begin()
    run(ticks[0])
    cot_block.begin()
    cross.begin()
    run(ticks[1])

    block.arrived()
    valid_swap.arrived()
    keeps[0].start()
    chunk = rows // 3

    def normalise(i, nothing):
        at = pl.ds(pl.multiple_of(i * chunk, 16), chunk)
        value, spread = standardize(x[at, :].astype(f32))
        hat[at, :] = value
        return nothing

    lax.fori_loop(0, 3, normalise, 0)
    flags = jnp.where(y == 0, valid_both[0:1, :], valid_both[1:2, :]).astype(f32)
    count = jnp.sum(flags, axis=1, keepdims=True)
    count_out[...] = jnp.broadcast_to(count, count_out.shape)
    columns = (count - 1.0) * (1.0 / grid_side)
    token = lax.broadcasted_iota(jnp.int32, (rows, lanes), 0).astype(f32)
    token = token + (k * tokens_here).astype(f32)
    lane = lax.broadcasted_iota(jnp.int32, (rows, lanes), 1)
    live = jnp.logical_and(token >= 1.0, token < count)
    row_id = jnp.floor((token - 0.5) / columns)
    col_id = token - 1.0 - row_id * columns
    where_at = jnp.where(lax.rem(lane, head_size) < 2 * quarter, row_id, col_id)
    where_at = jnp.where(live, where_at, 0.0)
    power = lax.rem(lane, quarter).astype(f32) * (-math.log(10000.0) / quarter)
    angle = where_at * jnp.exp(power)
    cos[...] = jnp.cos(angle)
    sin[...] = jnp.sin(angle)
    bias[...] = slot_bias(bias.shape, 1, rows, tokens_here, count)

    for tick in ticks[2:8]:
        run(tick)
    jobs[0].arrived()
    vec_load.start()
    vec_load.wait()
    piece_rows = vec_own.shape[0]
    summed = vec[0:piece_rows, :].astype(f32)
    for s in range(1, 2 * layers):
        summed = summed + vec[s * piece_rows : (s + 1) * piece_rows, :].astype(f32)
    vec_out[...] = summed

    def scale(i, nothing):
        at = pl.ds(pl.multiple_of(i * chunk, 16), chunk)
        normed[at, :] = (hat[at, :] * vec_out[4:5, :] + vec_out[6:7, :]).astype(bf16)
        return nothing

    lax.fori_loop(0, 3, scale, 0)
    keeps[1].start()
    repeat = tile // lanes
    per = width // tile
    for mat in range(3):
        run(ticks[8 + mat])
        jobs[1 + mat].arrived()
        for part in range(per):
            weight_loads[mat * per + part].start()
        for part in range(per):
            load = weight_loads[mat * per + part]
            load.wait()
            cols = pl.ds(part * tile, tile)
            raw = dot(normed[...], weight[(mat * per + part) % 2])
            if mat != 1:
                raw = raw + vec_out[0 if mat == 0 else 1 : 1 if mat == 0 else 2, cols]
            if mat < 2:
                turned = turn_lanes(raw, quarter)
                wide_cos = jnp.concatenate([cos[...]] * repeat, axis=1)
                wide_sin = jnp.concatenate([sin[...]] * repeat, axis=1)
                raw = raw * wide_cos + turned * wide_sin
            if mat == 0:
                q[:, cols] = raw.astype(bf16)
            else:
                (keys if mat == 1 else values)[my_rows, cols] = raw.astype(bf16)
                shares[(mat - 1) * per + part][0].start()
    keeps[2].start()
    for out_going, coming in shares:
        out_going.wait_send()
        coming.wait_recv()
    keeps[3].start()
    keeps[4].start()

    late = ticks[11:]
    score_scale = LOG2_E / math.sqrt(head_size)
    pairs = width // lanes

    def mix(i, nothing):
        for number, tick in enumerate(late):
            pl.when(i == number)(functools.partial(run, tick))
        cols = pl.ds(pl.multiple_of(i * lanes, lanes), lanes)
        queries, near_keys, near_values = q[:, cols], keys[:, cols], values[:, cols]
        parts = []
        for head in range(2):
            s = dot_last(only_head(queries, head, head_size), near_keys) * score_scale + bias[...]
            top = jnp.max(s, axis=1, keepdims=True)
            e = jnp.exp2(s - top)
            total = jnp.sum(e, axis=1, keepdims=True)
            parts.append(dot(e.astype(bf16), near_values) * (1.0 / total))
            level = jnp.broadcast_to(top + jnp.log2(total), (rows, 128))
            stat_out[i, head : head + 1, :] = jnp.transpose(level)[0:1, :]
        o_out[:, cols] = jnp.where(pair_lanes((rows, lanes), head_size), parts[0], parts[1])
        return nothing

    lax.fori_loop(0, pairs, mix, 0)
    for tick in late[8:]:
        run(tick)
    for job in jobs[4:]:
        job.arrived()
    cross.arrived()
    cot_block.arrived()
    for keep in keeps:
        keep.wait()
    links.finish()


def front(
    layers, number, head_size, grid_side, vec, qkv, out, gate, down, tokens, cot, valid, hidden
):
    bf16, f32 = jnp.bfloat16, jnp.float32
    rows, width = tokens.shape[1:]
    pairs = width // (2 * head_size)
    tile = 512
    fulls = [
        full_shape(layers, kind, piece.shape)
        for kind, piece in ((ROW, vec), (ROW, qkv), (COL, out), (ROW, gate), (COL, down))
    ]
    shapes = [jax.ShapeDtypeStruct(shape, bf16) for shape in fulls]
    shapes += [jax.ShapeDtypeStruct((2,) + hidden.shape, bf16)]
    shapes += [jax.ShapeDtypeStruct((n * rows, width), bf16) for n in (1, 1, 1, 1, 2, 2)]
    shapes += [
        jax.ShapeDtypeStruct((rows, width), f32),
        jax.ShapeDtypeStruct((pairs, 2, rows), f32),
        jax.ShapeDtypeStruct((vec.shape[0], width), f32),
        jax.ShapeDtypeStruct((8, 128), f32),
        jax.ShapeDtypeStruct((rows, 2 * head_size), f32),
        jax.ShapeDtypeStruct((rows, 2 * head_size), f32),
    ]
    sems = 11 * Gather.sem_count(layers) + 8
    return pl.pallas_call(
        functools.partial(front_kernel, layers, head_size, grid_side),
        out_shape=shapes,
        in_specs=[ANY] * 9,
        out_specs=[ANY] * 12 + [IN_VMEM] * 6,
        scratch_shapes=[
            pltpu.VMEM((rows, width), bf16),
            pltpu.VMEM(valid.shape, valid.dtype),
            pltpu.VMEM(fulls[0], bf16),
            pltpu.VMEM((2, width, tile), bf16),
            pltpu.VMEM((rows, width), f32),
            pltpu.VMEM((rows, width), bf16),
            pltpu.VMEM((rows, width), bf16),
            pltpu.VMEM((2 * rows, width), bf16),
            pltpu.VMEM((2 * rows, width), bf16),
            pltpu.VMEM((1, 2 * rows), f32),
            pltpu.SemaphoreType.DMA((sems,)),
            pltpu.SemaphoreType.DMA((sems,)),
            pltpu.SemaphoreType.DMA((32,)),
        ],
        compiler_params=pltpu.CompilerParams(
            collective_id=number, has_side_effects=True, vmem_limit_bytes=LIMIT
        ),
    )(vec, qkv, out, gate, down, tokens, cot, valid, hidden)


def back_kernel(layers, head_size, tokens_here, jobs, late_jobs, mats, *refs):
    grads, refs = refs[:mats], refs[mats:]
    given_arrays, refs = refs[:9], refs[9:]
    q_in, keys_in, values_in, do_in, mixed_in, n_in, x_in, resid_in, weights = given_arrays
    stats, count, cos, sin, vec, total_in = refs[:6]
    outs, refs = refs[6 : 6 + mats], refs[6 + mats :]
    late_outs, total_out, tokens_out, late_grads = refs[:3], refs[3], refs[4], refs[5:8]
    scratch, refs = refs[8 : 8 + 6 * len(jobs)], refs[8 + 6 * len(jobs) :]
    (
        q, keys, values, do, mixed, k_sum, v_sum, dq_low, dk_low, dv_low, normed_t, d_first,
        d_tokens, bias, total, boxes, layer_boxes, send_sem, recv_sem, local_sem, ready,
    ) = refs
    f32, bf16 = jnp.float32, jnp.bfloat16
    place = place_of()
    z, k, x, y = place
    greet(layers, place, (SWAP, FAR))
    links = Links(place, send_sem, recv_sem)
    first_jobs = reduce_jobs(layers, links, jobs, grads, outs, scratch, local_sem)
    locals_used = [len(jobs) * 2 * layers]

    def local_at():
        locals_used[0] += 1
        return local_sem.at[locals_used[0] - 1]

    second_jobs = []
    for mat, low, rows_here, split, host, first_col in late_jobs:
        cols_here = pl.ds(first_col, late_outs[mat].shape[-1])
        own = []
        for ref in scratch[6 * host : 6 * host + 6]:
            own.append(ref.at[(slice(None),) * (len(ref.shape) - 1) + (cols_here,)])
        second_jobs.append(
            Reduce(
                layers, links, ROW, late_grads[mat], late_outs[mat], low, split, own,
                local_sem, locals_used[0],
            )
        )
        locals_used[0] += 2 * layers
    sums = Total(layers, links, total, total_out, boxes, layer_boxes)
    early, n_late = len(jobs), len(second_jobs)
    handover = early + 5
    late_starts = [handover + number // 2 for number in range(n_late)]
    starts = list(range(early)) + late_starts + [handover + 3]
    begins = [max(0, number - 1) for number in range(early)] + late_starts + [handover + 3]
    ticks = ticks_of(links, first_jobs + second_jobs + [sums], starts, begins)
    spread = Spread(links, d_tokens, tokens_out, local_at())

    rows, width = q.shape
    lanes = 2 * head_size
    pairs = width // lanes
    scale = 1.0 / math.sqrt(head_size)
    quarter = head_size // 4
    my_rows = pl.ds(pl.multiple_of(k * rows, 16), rows)
    other_rows = pl.ds(pl.multiple_of((1 - k) * rows, 16), rows)
    first = links.take(2 * pairs)

    def share(i):
        cols = pl.ds(pl.multiple_of(i * lanes, lanes), lanes)
        return (
            links.copy(CORE, first + 2 * i, k_sum.at[other_rows, cols], dk_low.at[:, cols]),
            links.copy(CORE, first + 2 * i + 1, v_sum.at[other_rows, cols], dv_low.at[:, cols]),
        )

    def turn_back(grad):
        return grad * cos[...] - turn_lanes(grad, quarter) * sin[...]

    def load(source, target):
        copy = pltpu.make_async_copy(source, target, local_at())
        copy.start()
        return copy

    run(ticks[0])
    loads = [
        load(source, target)
        for source, target in (
            (q_in, q), (keys_in, keys), (values_in, values), (do_in, do), (mixed_in, mixed)
        )
    ]
    bias[...] = slot_bias(bias.shape, 0, rows, tokens_here, count[0:1, 0:1])
    total[...] = total_in[...]
    run(ticks[1])
    for copy in loads:
        copy.wait()
    beside = ticks[2 : 2 + pairs]

    def step(i, nothing):
        for number, tick in enumerate(beside):
            pl.when(i == number)(functools.partial(run, tick))
        cols = pl.ds(pl.multiple_of(i * lanes, lanes), lanes)
        queries, near_keys, near_values, grad = q[:, cols], keys[:, cols], values[:, cols], do[:, cols]
        products = jnp.transpose(grad.astype(f32) * mixed[:, cols])
        found = []
        for head in range(2):
            row_dot = products[head * head_size : (head + 1) * head_size]
            row_dot = jnp.sum(row_dot, axis=0, keepdims=True)
            s = dot_last(near_keys, only_head(queries, head, head_size)) * (scale * LOG2_E)
            p = jnp.exp2(s + bias[...] - stats[i, head : head + 1, :])
            dp = dot_last(near_values, only_head(grad, head, head_size))
            ds = (p * (dp - row_dot)).astype(bf16)
            found.append(
                (dot_first(near_keys, ds) * scale, dot(ds, queries) * scale, dot(p.astype(bf16), grad))
            )
        dq = jnp.concatenate([found[0][0][:head_size], found[1][0][head_size:]], axis=0)
        dq = turn_back(jnp.transpose(dq)).astype(bf16)
        dq_low[:, cols] = dq
        total[pl.ds(i, 1), :] = jnp.sum(dq.astype(f32), axis=0, keepdims=True)
        in_first = pair_lanes((2 * rows, lanes), head_size)
        k_sum[:, cols] = jnp.where(in_first, found[0][1], found[1][1]).astype(bf16)
        v_sum[:, cols] = jnp.where(in_first, found[0][2], found[1][2]).astype(bf16)
        for copy in share(i):
            copy.start()
        return nothing

    lax.fori_loop(0, pairs, step, 0)
    normed_load = load(n_in, q)
    loads = [load(weights.at[0], keys.at[pl.ds(0, width)]), load(weights.at[1], values.at[pl.ds(0, width)])]
    loads += [load(x_in, do), load(resid_in, mixed)]
    at_tick = [2 + pairs]

    def advance():
        run(ticks[at_tick[0]])
        at_tick[0] += 1

    def join(i, nothing):
        cols = pl.ds(pl.multiple_of(i * lanes, lanes), lanes)
        for copy in share(i):
            copy.wait()
        dk = k_sum[my_rows, cols].astype(f32) + dk_low[:, cols].astype(f32)
        dk_low[:, cols] = turn_back(dk).astype(bf16)
        dv = v_sum[my_rows, cols].astype(f32) + dv_low[:, cols].astype(f32)
        dv = dv.astype(bf16)
        dv_low[:, cols] = dv
        total[pl.ds(pairs + i, 1), :] = jnp.sum(dv.astype(f32), axis=0, keepdims=True)
        return nothing

    advance()
    lax.fori_loop(0, pairs, join, 0)
    normed_load.wait()
    last_weight = load(weights.at[2], k_sum.at[pl.ds(0, width)])

    def flip(i, nothing):
        at = pl.ds(pl.multiple_of(i * lanes, lanes), lanes)
        normed_t[at, :] = jnp.transpose(q[:, at])
        return nothing

    lax.fori_loop(0, width // lanes, flip, 0)
    while at_tick[0] < handover:
        advance()
    tile = 256
    stores = []

    def weight_grad(mat):
        low_grad = (dq_low, dk_low, dv_low)[mat]
        def part(i, nothing):
            at = pl.ds(pl.multiple_of(i * tile, tile), tile)
            v_sum[at, :] = dot(normed_t[at, :], low_grad[...]).astype(bf16)
            return nothing

        lax.fori_loop(0, width // tile, part, 0)
        stores.append(load(v_sum.at[pl.ds(0, width)], late_grads[mat]))

    weight_grad(0)
    for job in first_jobs[:4]:
        job.finish()
    near = [(None, CORE), (None, ACROSS), (None, BESIDE), (z > 0, DOWN), (z < layers - 1, UP)]
    for condition, way in near:

        def hello(way=way):
            pl.semaphore_signal(
                ready, inc=1, device_id=device(place, way), device_id_type=MESH
            )

        when(condition, hello)
    expected = 3 + jnp.where(z > 0, 1, 0) + jnp.where(z < layers - 1, 1, 0)
    pl.semaphore_wait(ready, expected)
    stores[-1].wait()
    advance()
    for mat in (1, 2):
        weight_grad(mat)
        stores[-1].wait()
        advance()
    for copy in loads + [last_weight]:
        copy.wait()

    def project_back(i, nothing):
        at = pl.ds(pl.multiple_of(i * tile, tile), tile)
        result = dot_last(dq_low[...], keys[at, :])
        result = result + dot_last(dk_low[...], values[at, :])
        d_first[:, at] = result + dot_last(dv_low[...], k_sum[at, :])
        return nothing

    lax.fori_loop(0, width // tile, project_back, 0)
    chunk = rows // 3
    gain = vec[4:5, :]
    gain_sum = jnp.zeros((1, width), f32)
    bias_sum = jnp.zeros((1, width), f32)
    for number in range(3):
        at = pl.ds(number * chunk, chunk)
        hat, inverse = standardize(do[at, :].astype(f32))
        dn = d_first[at, :]
        d_tokens[at, :] = (mixed[at, :] + norm_back(dn * gain, hat, inverse)).astype(bf16)
        gain_sum = gain_sum + jnp.sum(dn * hat, axis=0, keepdims=True)
        bias_sum = bias_sum + jnp.sum(dn, axis=0, keepdims=True)
    for i in range(width // 128):
        cols = slice(i * 128, (i + 1) * 128)
        at = 4 * width // 128 + i
        total[at : at + 1, :] = gain_sum[:, cols]
        at = 6 * width // 128 + i
        total[at : at + 1, :] = bias_sum[:, cols]
    spread.begin()
    while at_tick[0] < len(ticks):
        advance()
    spread.arrived()
    for job in first_jobs[4:] + second_jobs:
        job.finish()
    links.finish()


def back(layers, number, head_size, tokens_here, jobs, late_jobs, grads, given, small, total):
    bf16, f32 = jnp.bfloat16, jnp.float32
    pieces = [piece_shape(layers, kind, g.shape) for kind, g in grads]
    rows, width = given[0].shape
    pairs = width // (2 * head_size)
    sems = (len(jobs) + len(late_jobs)) * Reduce.sem_count(layers) + 2 * pairs
    sems += Total.sem_count(layers) + 2
    late_piece = (width // (2 * layers), width // 2)
    scratch = []
    for mat, kind, low, job_rows, split in jobs:
        shapes = reduce_shapes(layers, job_rows, pieces[mat][-1], split)
        scratch += [pltpu.VMEM(shape, bf16) for shape in shapes]
    half, whole = (rows, width), (2 * rows, width)
    buffers = [(half, bf16), (whole, bf16), (whole, bf16), (half, bf16), (half, f32)]
    buffers += [(whole, bf16)] * 2 + [(half, bf16)] * 3 + [((width, rows), bf16), (half, f32)]
    buffers += [(half, bf16), ((2 * rows, 1), f32), (total.shape, f32)]
    buffers += [((5,) + total.shape, f32), ((layers,) + total.shape, f32)]
    return pl.pallas_call(
        functools.partial(
            back_kernel, layers, head_size, tokens_here, jobs, late_jobs, len(grads)
        ),
        out_shape=[jax.ShapeDtypeStruct(piece, f32) for piece in pieces]
        + [jax.ShapeDtypeStruct(late_piece, f32)] * 3
        + [jax.ShapeDtypeStruct(total.shape, f32)]
        + [jax.ShapeDtypeStruct((2, rows, width), bf16)]
        + [jax.ShapeDtypeStruct((width, width), bf16)] * 3,
        in_specs=[ANY] * (len(grads) + len(given)) + [IN_VMEM] * (len(small) + 1),
        out_specs=[IN_VMEM] * (len(pieces) + 4) + [ANY] * 4,
        scratch_shapes=scratch
        + [pltpu.VMEM(shape, dtype) for shape, dtype in buffers]
        + [
            pltpu.SemaphoreType.DMA((sems,)),
            pltpu.SemaphoreType.DMA((sems,)),
            pltpu.SemaphoreType.DMA(((len(jobs) + len(late_jobs)) * 2 * layers + 16,)),
            pltpu.SemaphoreType.REGULAR,
        ],
        compiler_params=pltpu.CompilerParams(
            collective_id=number, has_side_effects=True, vmem_limit_bytes=62 * 1024 * 1024
        ),
    )(*[g for kind, g in grads], *given, *small, total)


def pad_to(values, axis, size):
    pads = [(0, 0)] * values.ndim
    pads[axis] = (0, size - values.shape[axis])
    return jnp.pad(values, pads)


def round_up(size, step):
    return (size + step - 1) // step * step


def image_per_chip(
    layers,
    tokens,
    cotangent,
    valid_tokens,
    places,
    qkv_weight,
    head_biases,
    head_gain,
    out_weight,
    norm_gains,
    width_biases,
    gate_up,
    hidden_biases,
    hidden_gain,
    down_weight,
):
    f32 = jnp.float32
    bf16 = jnp.bfloat16
    z, k, x, y = place_of()
    s = 2 * z + k
    shards = 2 * layers
    width = tokens.shape[2]
    rows = tokens.shape[1]
    heads_here = head_gain.shape[0]
    heads = 2 * heads_here
    dims_here = head_gain.shape[1]
    head_size = dims_here * shards
    real_here = hidden_gain.shape[0]
    hidden_here = round_up(real_here, 128)
    real = 2 * real_here
    hidden_size = 2 * hidden_here
    score_scale = 1.0 / math.sqrt(head_size)

    padded = round_up(rows, 16)
    heads_own = jnp.concatenate([head_biases, head_gain[None]], axis=0)
    spot = jnp.zeros((4, heads_here, head_size), bf16)
    spot = lax.dynamic_update_slice(spot, heads_own, (0, 0, s * dims_here)).reshape(4, -1)
    width_own = jnp.concatenate([norm_gains, width_biases], axis=0)
    lane_at = s * width_own.shape[1] - y * spot.shape[1]
    inside = both(lane_at >= 0, lane_at < spot.shape[1])
    width_own = jnp.where(inside, width_own, jnp.zeros_like(width_own))
    at = jnp.where(inside, lane_at, 0)
    lanes_own = lax.dynamic_update_slice(jnp.zeros((6, spot.shape[1]), bf16), width_own, (0, at))
    vectors = pad_to(jnp.concatenate([spot, lanes_own], axis=0), 0, 16)
    hidden_vectors = jnp.concatenate([hidden_biases, hidden_gain[None]], axis=0)
    hidden_vectors = pad_to(pad_to(hidden_vectors, 1, hidden_here), 0, 16)
    gate_pad = pad_to(gate_up, 2, hidden_here)
    down_pad = pad_to(down_weight, 0, hidden_here)
    swaps, others = [], []
    for layer in range(layers):
        swaps += [(4 * layer + 1, 4 * layer + 2), (4 * layer + 2, 4 * layer + 1)]
        for spot, far in ((0, 0), (1, 2), (2, 1), (3, 3)):
            for side in range(2):
                others.append((2 * (4 * layer + spot) + side, 2 * (4 * layer + far) + 1 - side))
    (
        vec_full, qkv_full, out_full, gate_full, down_full, hidden_full, cot_block,
        token_block, first_in, queries, keys, values, mixed, stats, vec, count, cos, sin,
    ) = front(
        layers, 0, head_size, 32, vectors, qkv_weight, out_weight, gate_pad, down_pad,
        pad_to(tokens, 1, padded), pad_to(cotangent, 1, padded), valid_tokens, hidden_vectors,
    )
    head_part, norm_scale, width_bias = vec[0:4], vec[4:6], vec[6:10]
    hidden_part = jnp.concatenate([hidden_full[0, :4], hidden_full[1, :4]], axis=1).astype(f32)
    token_rows = token_block.astype(f32)
    cot_rows = cot_block.astype(f32)
    mix_hat, spread_mix = standardize(mixed)
    mix_in = (mix_hat * head_part[3] + head_part[2]).astype(bf16)
    branch = jnp.dot(mix_in, out_full, preferred_element_type=f32)
    resid = token_rows + (branch + width_bias[2])
    normed_two, spread_two = standardize(resid)
    second_in = (normed_two * norm_scale[1] + width_bias[1]).astype(bf16)
    gate_pre = jnp.dot(second_in, gate_full[0], preferred_element_type=f32) + hidden_part[0]
    up_pre = jnp.dot(second_in, gate_full[1], preferred_element_type=f32) + hidden_part[1]
    sigmoid_gate = jax.nn.sigmoid(gate_pre)
    silu_gate = gate_pre * sigmoid_gate
    hidden = silu_gate * up_pre
    hidden_mean = jnp.sum(hidden, axis=-1, keepdims=True) / real
    centred = hidden - hidden_mean
    extra = (hidden_size - real) * hidden_mean * hidden_mean
    hidden_var = (jnp.sum(centred * centred, axis=-1, keepdims=True) - extra) / real
    spread_hid = lax.rsqrt(jnp.maximum(hidden_var, 0.0) + EPS)
    hidden_hat = centred * spread_hid
    down_in = (hidden_hat * hidden_part[3] + hidden_part[2]).astype(bf16)
    ffn_out = jnp.dot(down_in, down_full, preferred_element_type=f32)
    result = (resid + (ffn_out + width_bias[3])).astype(bf16)[:rows]
    result_other = lax.ppermute(result, (SHARD, CTX, TP), others)
    results = (result, result_other, lax.ppermute(result, (SHARD, CTX), swaps))

    g_down = jnp.einsum("tf,td->fd", down_in, cot_block, preferred_element_type=f32)
    d_down_in = jnp.einsum("td,fd->tf", cot_block, down_full, preferred_element_type=f32)
    grad_hid = d_down_in * hidden_part[3]
    hid_back_one = jnp.sum(grad_hid, axis=-1, keepdims=True) / real
    hid_back_two = jnp.sum(grad_hid * hidden_hat, axis=-1, keepdims=True) / real
    d_hidden = (grad_hid - hid_back_one - hidden_hat * hid_back_two) * spread_hid
    d_gate = (d_hidden * up_pre * sigmoid_gate * (1.0 + gate_pre * (1.0 - sigmoid_gate))).astype(
        bf16
    )
    d_up = (d_hidden * silu_gate).astype(bf16)
    g_gate = jnp.einsum("td,tf->df", second_in, d_gate, preferred_element_type=f32).astype(bf16)
    g_up = jnp.einsum("td,tf->df", second_in, d_up, preferred_element_type=f32).astype(bf16)
    d_second = jnp.einsum("tf,df->td", d_gate, gate_full[0], preferred_element_type=f32)
    d_second = d_second + jnp.einsum("tf,df->td", d_up, gate_full[1], preferred_element_type=f32)
    d_resid = cot_rows + norm_back(d_second * norm_scale[1], normed_two, spread_two)
    d_branch_low = d_resid.astype(bf16)
    g_out = jnp.einsum("tm,tn->mn", mix_in, d_branch_low, preferred_element_type=f32)
    d_mix_in = jnp.einsum("tn,mn->tm", d_branch_low, out_full, preferred_element_type=f32)
    d_mixed = norm_back(d_mix_in * head_part[3], mix_hat, spread_mix).astype(bf16)
    vector_grads = jnp.concatenate(
        [
            jnp.zeros((width,), f32),
            jnp.zeros((width,), f32),
            column_sum(d_mix_in),
            column_sum(d_mix_in * mix_hat),
            jnp.zeros((width,), f32),
            column_sum(d_second * normed_two),
            jnp.zeros((width,), f32),
            column_sum(d_second),
            column_sum(d_branch_low),
            column_sum(cot_block),
            column_sum(d_gate),
            column_sum(d_up),
            column_sum(d_down_in),
            column_sum(d_down_in * hidden_hat),
        ]
    ).reshape(-1, 128)
    vector_grads = pad_to(vector_grads, 0, round_up(vector_grads.shape[0], 16))
    result, result_other, swapped, d_mixed = lax.optimization_barrier((*results, d_mixed))
    result = jnp.where(k == x, result, swapped)
    result = jnp.stack(
        [jnp.where(y == 0, result, result_other), jnp.where(y == 0, result_other, result)], axis=1
    ).transpose(1, 0, 2)
    half = hidden_here // 2
    heads_rows = heads_here * head_size
    grad_jobs = (
        (0, ROW, 0, 64, 32), (0, ROW, 64, 64, 32), (1, ROW, 0, 64, 32), (1, ROW, 64, 64, 32),
        (2, COL, 0, half, half // 2), (2, COL, half, half, half // 2),
        (3, COL, 0, heads_rows, heads_rows // 2),
    )
    late_jobs = (
        (0, 0, 64, 32, 0, 0), (0, 64, 64, 32, 1, 0),
        (1, 0, 64, 32, 0, heads_rows), (1, 64, 64, 32, 1, heads_rows),
        (2, 0, 64, 32, 2, 0), (2, 64, 64, 32, 3, 0),
    )
    back_grads = (
        (ROW, g_gate), (ROW, g_up), (COL, g_down.astype(bf16)), (COL, g_out.astype(bf16))
    )
    (
        gate_piece, up_piece, down_piece, out_piece, query_piece, key_piece, value_piece,
        vector_grads, d_tokens, *unused,
    ) = back(
        layers, 1, head_size, rows, grad_jobs, late_jobs, back_grads,
        (queries, keys, values, d_mixed, mixed, first_in, token_block, d_resid, qkv_full),
        (stats, count, cos, sin, vec), vector_grads,
    )
    d_tokens = jnp.stack([d_tokens[0, :rows], d_tokens[1, :rows]], axis=1).transpose(1, 0, 2)
    vector_grads = vector_grads.reshape(-1)
    head_sums = vector_grads[: 4 * width].reshape(4, heads, head_size)
    head_sums = lax.dynamic_slice(
        head_sums, (0, y * heads_here, s * dims_here), (4, heads_here, dims_here)
    )
    width_sums = vector_grads[4 * width : 10 * width].reshape(6, width)
    width_sums = lax.dynamic_slice(width_sums, (0, s * 128), (6, width // shards))
    hidden_sums = vector_grads[10 * width : 10 * width + 4 * hidden_size]
    hidden_sums = hidden_sums.reshape(4, hidden_size)
    hidden_sums = lax.dynamic_slice(hidden_sums, (0, y * hidden_here), (4, hidden_here))
    hidden_sums = hidden_sums[:, :real_here]

    return (
        result,
        d_tokens.astype(f32),
        jnp.stack([query_piece, key_piece, value_piece]),
        head_sums[:3],
        head_sums[3],
        out_piece,
        width_sums[:2],
        width_sums[2:],
        jnp.stack([gate_piece[:, :real_here], up_piece[:, :real_here]]),
        hidden_sums[:3],
        hidden_sums[3],
        down_piece[:real_here],
    )


def solution(mesh):
    small = mesh.shape[CTX] == 2 and mesh.shape[TP] == 2
    body = functools.partial(image_per_chip, mesh.shape[SHARD] // 2) if small else general_plan

    return jax.shard_map(
        body,
        mesh=mesh,
        in_specs=(
            P(SHARD, CTX, None),
            P(SHARD, CTX, None),
            P(SHARD, None),
            P(None, SHARD, CTX),
            P(None, SHARD, TP),
            P(None, TP, SHARD),
            P(TP, SHARD),
            P(TP, SHARD),
            P(None, SHARD),
            P(None, SHARD),
            P(None, SHARD, TP),
            P(None, TP),
            P(TP),
            P(TP, SHARD),
        ),
        out_specs=(
            P(SHARD, CTX, None),
            P(SHARD, CTX, None),
            P(None, SHARD, TP),
            P(None, TP, SHARD),
            P(TP, SHARD),
            P(TP, SHARD),
            P(None, SHARD),
            P(None, SHARD),
            P(None, SHARD, TP),
            P(None, TP),
            P(TP),
            P(TP, SHARD),
        ),
        check_vma=False,
    )
```

profile of v0, /device:TPU:0, one launch (start us, length us, event | category | flops | bytes accessed | tf_op | source)
XLA Modules:
  0.0 476.1 jit_solution(13227415512352890781)
XLA Ops:
  3.8 1.7 pad.33.refs_4_
  5.6 2.3 copy.25
  9.5 1.5 pad.34.refs_5_
  12.5 1.6 pad.35.refs_6_
  14.7 139.7 %shard_map.220 = (bf16[128,1024]{1,0:T(8,128)(2,1)}, bf16[3,1024,1024]{2,1,0:T(8,128)(2,1)}, bf16[1024,1024]{1,0:T(8,128)(2,1)}, bf16[2,1024,2816]{2,1,0:T(8,128...) custom-call(bf16[16,512]{1,0:T(8,128)(2,1)} %fusion.21.refs_0_, ...), custom_call_target="tpu_custom_call" | custom-call | tf_op jit(solution)/shard_map/pallas_call | solution.py:1301
  155.3 1.9 reduce_sum.198
  157.8 1.1 fusion.29
  158.9 3.2 fusion.30
  163.0 3.2 fusion.7
  166.3 11.0 %fusion.28 = (f32[528]{0:T(1024)S(1)}, f32[528,2816]{1,0:T(8,128)S(1)}, f32[528,2816]{1,0:T(8,128)}) fusion(f32[2816]{0:T(1024)S(1)} %get-tuple-element.98, f32[528,2816]{1,0:T(8,128)S(1)} %fusion.7, f32[2816]{0:T(1024)S(1)} %get-tuple-element.99, bf16[528,1024]{1,0:T(8,128)(2,1)S(1)} %add_convert_fusion.1, bf16[2,1024,2816]{2,1,0:T(8,128)(2,1)} %get-tuple-element.46), kind=kOutput, calls=%fused_computation.114 | convolution fusion | flops 3056958976 | bytes 24715328 | tf_op jit(solution)/shard_map/dot_general | solution.py:1669
  178.0 1.8 copy-done.3
  179.8 3.5 fusion.27
  183.8 1.7 collective-permute-start.1
  186.4 11.2 %multiply_reduce_fusion = (f32[2816]{0:T(1024)S(1)}, f32[528]{0:T(1024)S(1)}, f32[528]{0:T(1024)S(1)}, f32[2816]{0:T(1024)S(1)}, f32[528,2816]{1,0:T(8,128)}) fusion(f32[528,2816]{1,0:T(8,128)} %copy-done.3, f32[528]{0:T(1024)S(1)} %add_rsqrt_fusion, f32[528]{0:T(1024)S(1)} %broadcast_multiply_fusion.2, f32[2816]{0:T(1024)S(1)} %get-tuple-element.96, ...), kind=kOutput, calls=%fused_computation | convolution fusion | flops 3058439680 | bytes 18785536 | tf_op jit(solution)/shard_map/td,fd->tf/dot_general | solution.py:1686
  197.6 8.2 %convert_reduce_fusion.1 = (f32[2816]{0:T(1024)S(1)}, bf16[528,2816]{1,0:T(8,128)(2,1)}, f32[2816]{0:T(1024)S(1)}, bf16[528,2816]{1,0:T(8,128)(2,1)S(1)}) fusion(f32[528,2816]{1,0:T(8,128)S(1)} %bitcast.66, f32[2816]{0:T(1024)S(1)} %get-tuple-element.99, f32[528,2816]{1,0:T(8,128)S(1)} %bitcast.68, f32[2816]{0:T(1024)S(1)} %get-tuple-element.98, ...), kind=kLoop, calls=%fused_computation.2 | loop fusion | flops 38652416 | bytes 29801728 | tf_op jit(solution)/shard_map/reduce_sum | solution.py:60
  205.8 6.4 %fusion.1 = f32[528,1024]{1,0:T(8,128)S(1)} fusion(bf16[528,2816]{1,0:T(8,128)(2,1)S(1)} %get-tuple-element.109, bf16[2,1024,2816]{2,1,0:T(8,128)(2,1)} %get-tuple-element.46), kind=kOutput, calls=%fused_computation.11 | convolution fusion | flops 3045064704 | bytes 10903552 | tf_op jit(solution)/shard_map/tf,df->td/dot_general | solution.py:1698
  212.3 6.2 %multiply_reduce_fusion.4 = (f32[1024]{0:T(1024)S(1)}, f32[528]{0:T(1024)S(1)}, f32[528]{0:T(1024)S(1)}, f32[1024]{0:T(1024)S(1)}, f32[528,1024]{1,0:T(8,128)S(1)}) fusion(f32[528,1024]{1,0:T(8,128)S(1)} %copy-done.2, f32[528]{0:T(1024)S(1)} %add_rsqrt_fusion.1, f32[528]{0:T(1024)S(1)} %broadcast_multiply_fusion.7, f32[1024]{0:T(1024)S(1)} %bitcast.74, ...), kind=kOutput, calls=%fused_computation.33 | convolution fusion | flops 3050468352 | bytes 15249664 | tf_op jit(solution)/shard_map/tf,df->td/dot_general | solution.py:1697
  218.6 1.0 convert_reduce_fusion.3
  220.2 3.0 multiply_reduce_fusion.5
  223.1 3.3 convolution_convert_fusion.3.refs_3_
  226.5 6.5 %convolution_convert_fusion.2.refs_0_ = bf16[1024,2816]{1,0:T(8,128)(2,1)} fusion(bf16[528,1024]{1,0:T(8,128)(2,1)S(1)} %copy-done.14, bf16[528,2816]{1,0:T(8,128)(2,1)S(1)} %copy-done.8), kind=kOutput, calls=%fused_computation.21 | convolution fusion | flops 3047948288 | bytes 9822208 | tf_op jit(solution)/shard_map/td,tf->df/dot_general | solution.py:1695
  233.0 6.9 %convolution_convert_fusion.1.refs_1_ = bf16[1024,2816]{1,0:T(8,128)(2,1)} fusion(bf16[528,1024]{1,0:T(8,128)(2,1)S(1)} %copy-done.14, bf16[528,2816]{1,0:T(8,128)(2,1)S(1)} %copy-done.7), kind=kOutput, calls=%fused_computation.20 | convolution fusion | flops 3047948288 | bytes 9822208 | tf_op jit(solution)/shard_map/td,tf->df/dot_general | solution.py:1696
  240.0 3.2 multiply_convert_fusion.2.refs_7_
  243.9 10.4 %convolution_convert_fusion.refs_2_ = bf16[2816,1024]{1,0:T(8,128)(2,1)} fusion(bf16[528,1024]{1,0:T(8,128)(2,1)} %get-tuple-element.49, f32[528,2816]{1,0:T(8,128)} %copy-done.3, f32[2816]{0:T(1024)S(1)} %get-tuple-element.97, f32[2816]{0:T(1024)S(1)} %get-tuple-element.96, f32[528]{0:T(1024)S(1)} %add_rsqrt_fusion, f32[528]{0:T(1024)S(1)} %broadcast_multiply_fusion.2), kind=kOutput, calls=%fused_computation.19 | convolution fusion | flops 3055382528 | bytes 12822656 | tf_op jit(solution)/shard_map/tf,td->fd/dot_general | solution.py:1685
  254.2 197.1 %shard_map.221 = (f32[128,1408]{1,0:T(8,128)}, f32[128,1408]{1,0:T(8,128)}, f32[1408,128]{1,0:T(8,128)}, f32[512,128]{1,0:T(8,128)}, f32[128,512]{1,0:T(8,128)},...) custom-call(bf16[1024,2816]{1,0:T(8,128)(2,1)} %convolution_convert_, ...), custom_call_target="tpu_custom_call" | custom-call | tf_op jit(solution)/shard_map/pallas_call | solution.py:1561
  457.5 1.4 select_bitcast_fusion.1
  459.2 3.5 copy.28
  462.7 1.1 slice_bitcast_fusion.1
  465.4 2.1 copy.30
  467.5 1.5 convert_bitcast_fusion
  469.0 5.3 %copy.29 = f32[2,516,1024]{2,0,1:T(2,128)} copy(f32[2,516,1024]{2,1,0:T(8,128)S(1)} %convert_bitcast_fusion) | data formatting | bytes 8454144
  474.3 0.9 pad_maximum_fusion.1
  (146 shorter events, 21.2 us)
Async XLA Ops:
  0.6 8.2 %copy-start.9 = (bf16[2,516,1024]{2,0,1:T(2,128)(2,1)S(1)}, bf16[2,516,1024]{2,0,1:T(2,128)(2,1)}, u32[]{:S(2)}) copy-start(bf16[2,516,1024]{2,0,1:T(2,128)(2,1)} %param.14) | copy-start | bytes 6340612
  154.4 2.8 copy-start
  155.3 3.6 copy-start.12
  157.2 5.7 %slice-start.6 = ((s8[11534336]{0:T(1024)(128)(4,1)}), s8[4194304]{0:T(1024)(128)(4,1)S(1)}, s32[]{:S(2)}) async-start(s8[11534336]{0:T(1024)(128)(4,1)} %bitcast.86), calls=%async_computation.6 | async-start | bytes 8388608
  158.9 4.1 slice-start.7
  158.9 4.1 slice-start.8
  162.1 21.2 %copy-start.1 = (f32[528,1024]{1,0:T(8,128)}, f32[528,1024]{1,0:T(8,128)S(1)}, u32[]{:S(2)}) copy-start(f32[528,1024]{1,0:T(8,128)S(1)} %get-tuple-element.124) | copy-start | bytes 6488068
  162.9 3.3 copy-start.13
  163.0 16.8 %slice-start.9 = ((s8[5767168]{0:T(1024)(128)(4,1)}), s8[4194304]{0:T(1024)(128)(4,1)S(1)}, s32[]{:S(2)}) async-start(s8[5767168]{0:T(1024)(128)(4,1)} %bitcast.88), calls=%async_computation.9 | async-start | bytes 8388608
  166.3 11.0 %copy-start.5 = (f32[528,2816]{1,0:T(8,128)}, f32[528,2816]{1,0:T(8,128)S(1)}, u32[]{:S(2)}) copy-start(f32[528,2816]{1,0:T(8,128)S(1)} %fusion.7) | copy-start | bytes 17842180
  166.3 13.5 %slice-start.10 = ((s8[5767168]{0:T(1024)(128)(4,1)}), s8[1572864]{0:T(1024)(128)(4,1)S(1)}, s32[]{:S(2)}) async-start(s8[5767168]{0:T(1024)(128)(4,1)} %bitcast.88), calls=%async_computation.10 | async-start | bytes 3145728
  177.3 2.5 copy-start.3
  183.8 70.4 %collective-permute-start.1 = (bf16[516,1024]{1,0:T(8,128)(2,1)S(1)}, bf16[516,1024]{1,0:T(8,128)(2,1)}, u32[]{:S(2)}, u32[]{:S(2)}) collective-permute-start(bf16[516,1024]{1,0:T(8,128)(2,1)S(1)} %fusion.13), channel_id=1, source_target_pairs={{2,4},{4,2},{10,12},{12,10},{18,20},{20,18},{26,28},{28,26},{3,5},... | collective-permute-start | bytes 3170312 | tf_op jit(solution)/shard_map/ppermute | solution.py:1683
  185.5 68.7 %collective-permute-start = (bf16[516,1024]{1,0:T(8,128)(2,1)S(1)}, bf16[516,1024]{1,0:T(8,128)(2,1)}, u32[]{:S(2)}, u32[]{:S(2)}) collective-permute-start(bf16[516,1024]{1,0:T(8,128)(2,1)S(1)} %fusion.13), channel_id=1, source_target_pairs={{0,1},{1,0},{2,5},{3,4},{4,3},{5,2},{6,7},{7,6},{8,9},{9,8},{10,13... | collective-permute-start | bytes 3170312 | tf_op jit(solution)/shard_map/ppermute | solution.py:1682
  186.3 11.2 %slice-start = ((s8[5947392]{0:T(1024)(128)(4,1)}), s8[4194304]{0:T(1024)(128)(4,1)S(1)}, s32[]{:S(2)}) async-start(s8[5947392]{0:T(1024)(128)(4,1)} %bitcast.63), calls=%async_computation | async-start | bytes 8388608
  186.3 11.2 %slice-start.2 = ((s8[5947392]{0:T(1024)(128)(4,1)}), s8[4194304]{0:T(1024)(128)(4,1)S(1)}, s32[]{:S(2)}) async-start(s8[5947392]{0:T(1024)(128)(4,1)} %bitcast.65), calls=%async_computation.2 | async-start | bytes 8388608
  186.3 11.2 %slice-start.4 = ((s8[5947392]{0:T(1024)(128)(4,1)}), s8[4194304]{0:T(1024)(128)(4,1)S(1)}, s32[]{:S(2)}) async-start(s8[5947392]{0:T(1024)(128)(4,1)} %bitcast.67), calls=%async_computation.4 | async-start | bytes 8388608
  186.4 11.2 %slice-start.1 = ((s8[5947392]{0:T(1024)(128)(4,1)}), s8[1753088]{0:T(1024)(128)(4,1)S(1)}, s32[]{:S(2)}) async-start(s8[5947392]{0:T(1024)(128)(4,1)} %bitcast.63), calls=%async_computation.1 | async-start | bytes 3506176
  186.4 11.2 %slice-start.3 = ((s8[5947392]{0:T(1024)(128)(4,1)}), s8[1753088]{0:T(1024)(128)(4,1)S(1)}, s32[]{:S(2)}) async-start(s8[5947392]{0:T(1024)(128)(4,1)} %bitcast.65), calls=%async_computation.3 | async-start | bytes 3506176
  186.4 11.2 %slice-start.5 = ((s8[5947392]{0:T(1024)(128)(4,1)}), s8[1753088]{0:T(1024)(128)(4,1)S(1)}, s32[]{:S(2)}) async-start(s8[5947392]{0:T(1024)(128)(4,1)} %bitcast.67), calls=%async_computation.5 | async-start | bytes 3506176
  205.8 6.4 %copy-start.6 = (bf16[528,2816]{1,0:T(8,128)(2,1)}, bf16[528,2816]{1,0:T(8,128)(2,1)S(1)}, u32[]{:S(2)}) copy-start(bf16[528,2816]{1,0:T(8,128)(2,1)S(1)} %get-tuple-element.109) | copy-start | bytes 8921092
  205.8 6.5 %copy-start.2 = (f32[528,1024]{1,0:T(8,128)S(1)}, f32[528,1024]{1,0:T(8,128)}, u32[]{:S(2)}) copy-start(f32[528,1024]{1,0:T(8,128)} %copy-done.1) | copy-start | bytes 6488068
  205.8 6.5 %copy-start.8 = (bf16[528,2816]{1,0:T(8,128)(2,1)S(1)}, bf16[528,2816]{1,0:T(8,128)(2,1)}, u32[]{:S(2)}) copy-start(bf16[528,2816]{1,0:T(8,128)(2,1)} %get-tuple-element.103) | copy-start | bytes 8921092
  212.3 6.3 %copy-start.15 = (bf16[528,1024]{1,0:T(8,128)(2,1)S(1)}, bf16[528,1024]{1,0:T(8,128)(2,1)}, u32[]{:S(2)}) copy-start(bf16[528,1024]{1,0:T(8,128)(2,1)} %get-tuple-element.49) | copy-start | bytes 3244036
  219.5 3.6 copy-start.4
  223.1 3.3 copy-start.14
  226.4 6.5 %copy-start.7 = (bf16[528,2816]{1,0:T(8,128)(2,1)S(1)}, bf16[528,2816]{1,0:T(8,128)(2,1)}, u32[]{:S(2)}) copy-start(bf16[528,2816]{1,0:T(8,128)(2,1)} %copy-done.6) | copy-start | bytes 8921092
  459.2 3.5 copy-start.11
  469.0 5.3 %copy-start.20 = (f32[128,512]{1,0:T(8,128)S(1)}, f32[128,512]{1,0:T(8,128)}, u32[]{:S(2)}) copy-start(f32[128,512]{1,0:T(8,128)} %get-tuple-element.64) | copy-start | bytes 786436
  469.0 5.3 %copy-start.21 = (f32[128,512]{1,0:T(8,128)S(1)}, f32[128,512]{1,0:T(8,128)}, u32[]{:S(2)}) copy-start(f32[128,512]{1,0:T(8,128)} %get-tuple-element.65) | copy-start | bytes 786436
  469.0 5.3 %copy-start.22 = (f32[128,512]{1,0:T(8,128)S(1)}, f32[128,512]{1,0:T(8,128)}, u32[]{:S(2)}) copy-start(f32[128,512]{1,0:T(8,128)} %get-tuple-element.66) | copy-start | bytes 786436
  469.0 6.2 %copy-start.19 = (f32[512,128]{1,0:T(8,128)S(1)}, f32[512,128]{1,0:T(8,128)}, u32[]{:S(2)}) copy-start(f32[512,128]{1,0:T(8,128)} %get-tuple-element.148) | copy-start | bytes 786436
  (7 other events, 11.8 us)
where the time goes:
time: 481 us; the launch traced here: 476 us
  Pallas kernels  337 us (70%)
  matrix products  74.8 us (16%)
  local copies, waits for them, and re-layouts  37.6 us (8%)
  other arithmetic  22.9 us (5%)
    pallas_call x1, Pallas kernels, back(): pl.pallas_call(functools.partial(back_kernel, layers, head_size, tokens_h...  197 us
    pallas_call x1, Pallas kernels, front(): pl.pallas_call(functools.partial(front_kernel, layers, head_size, grid_si...  140 us
    unnamed x93, local copies, waits for them, and re-layouts  19 us
    dot_general x1, matrix products, image_per_chip(): jnp.einsum('td,fd->tf', cot_block, down_full, preferred_element_type=f32)  11.2 us
    dot_general x1, matrix products, image_per_chip(): jnp.dot(second_in, gate_full[1], preferred_element_type=f32)  11 us
    dot_general x1, matrix products, image_per_chip(): jnp.einsum('tf,td->fd', down_in, cot_block, preferred_element_type=f32)  10.4 us
  transfers between devices with their start and end apart: 2, of which 0 were waited for; matrix products, arithmetic and copies ran while one was open for 14% of the time, Pallas kernels for 0%

commit v1 on v0

--- a/solution.py
+++ b/solution.py
@@ -1677,6 +1677,7 @@
     spread_hid = lax.rsqrt(jnp.maximum(hidden_var, 0.0) + EPS)
     hidden_hat = centred * spread_hid
     down_in = (hidden_hat * hidden_part[3] + hidden_part[2]).astype(bf16)
+    down_in = lax.optimization_barrier(down_in)
     ffn_out = jnp.dot(down_in, down_full, preferred_element_type=f32)
     result = (resid + (ffn_out + width_bias[3])).astype(bf16)[:rows]
     result_other = lax.ppermute(result, (SHARD, CTX, TP), others)

time: 481 us -> 469 us (0.975)
  matrix products: 74.8 us -> 66.5 us
    unnamed x93 -> x85, local copies, waits for them, and re-layouts: 19 us -> 17.5 us
  transfers between devices with their start and end apart: 2 -> 2, of which waited for: 0 -> 0; matrix products, arithmetic and copies ran while one was open for 14% -> 9% of each run, Pallas kernels for 0% -> 0%
where the time goes in v1:
time: 469 us; the launch traced here: 465 us
  Pallas kernels  337 us (72%)
  matrix products  66.5 us (14%)
  local copies, waits for them, and re-layouts  36.1 us (8%)
  other arithmetic  21.8 us (5%)
    pallas_call x1, Pallas kernels, back(): pl.pallas_call(functools.partial(back_kernel, layers, head_size, tokens_h...  197 us
    pallas_call x1, Pallas kernels, front(): pl.pallas_call(functools.partial(front_kernel, layers, head_size, grid_si...  140 us
    unnamed x85, local copies, waits for them, and re-layouts  17.5 us
    reduce_sum x2, other arithmetic, column_sum(): return jnp.sum(values.astype(jnp.float32), axis=0)  9.76 us
  transfers between devices with their start and end apart: 2, of which 0 were waited for; matrix products, arithmetic and copies ran while one was open for 9% of the time, Pallas kernels for 0%

profile of v1, /device:TPU:0, one launch (start us, length us, event | category | flops | bytes accessed | tf_op | source)
XLA Modules:
  0.0 464.9 jit_solution(8183224442249507427)
XLA Ops:
  1.6 2.2 copy.26
  3.9 1.5 pad.34.refs_5_
  6.9 1.6 pad.35.refs_6_
  8.5 1.0 copy.25
  9.5 0.9 pad.32.refs_3_
  12.5 139.7 %shard_map.220 = (bf16[128,1024]{1,0:T(8,128)(2,1)}, bf16[3,1024,1024]{2,1,0:T(8,128)(2,1)}, bf16[1024,1024]{1,0:T(8,128)(2,1)}, bf16[2,1024,2816]{2,1,0:T(8,128...) custom-call(bf16[16,512]{1,0:T(8,128)(2,1)} %fusion.21.refs_0_, ...), custom_call_target="tpu_custom_call" | custom-call | tf_op jit(solution)/shard_map/pallas_call | solution.py:1301
  153.4 1.9 reduce_sum.198
  155.7 1.1 fusion.28
  156.8 3.2 fusion.29
  160.8 3.3 fusion.7
  164.1 6.7 %fusion.27 = (f32[528]{0:T(1024)S(1)}, f32[528,2816]{1,0:T(8,128)S(1)}, f32[528,2816]{1,0:T(8,128)S(1)}) fusion(f32[2816]{0:T(1024)S(1)} %get-tuple-element.98, f32[528,2816]{1,0:T(8,128)S(1)} %fusion.7, f32[2816]{0:T(1024)S(1)} %get-tuple-element.99, bf16[528,1024]{1,0:T(8,128)(2,1)S(1)} %add_convert_fusion.1, bf16[2,1024,2816]{2,1,0:T(8,128)(2,1)} %get-tuple-element.46), kind=kOutput, calls=%fused_computation.113 | convolution fusion | flops 3056958976 | bytes 24715328 | tf_op jit(solution)/shard_map/dot_general | solution.py:1669
  172.0 9.2 %multiply_reduce_fusion = (f32[2816]{0:T(1024)S(1)}, f32[528]{0:T(1024)S(1)}, f32[528]{0:T(1024)S(1)}, f32[2816]{0:T(1024)S(1)}, f32[528,2816]{1,0:T(8,128)}) fusion(f32[528,2816]{1,0:T(8,128)S(1)} %get-tuple-element.107, f32[528]{0:T(1024)S(1)} %add_rsqrt_fusion, f32[528]{0:T(1024)S(1)} %broadcast_multiply_fusion.2, f32[2816]{0:T(1024)S(1)} %get-tuple-element.96, ...), kind=kOutput, calls=%fused_computation | convolution fusion | flops 3058439680 | bytes 18785536 | tf_op jit(solution)/shard_map/td,fd->tf/dot_general | solution.py:1687
  181.2 8.8 %convert_reduce_fusion.1 = (f32[2816]{0:T(1024)S(1)}, bf16[528,2816]{1,0:T(8,128)(2,1)S(1)}, f32[2816]{0:T(1024)S(1)}, bf16[528,2816]{1,0:T(8,128)(2,1)S(1)}, bf16[528,2816]{1,0:T(8,128)(2,1)}) fusion(f32[528,2816]{1,0:T(8,128)S(1)} %fusion.7, f32[2816]{0:T(1024)S(1)} %get-tuple-element.99, f32[528,2816]{1,0:T(8,128)S(1)} %get-tuple-element.126, ...), kind=kLoop, calls=%fused_computation.2 | loop fusion | flops 43112960 | bytes 32786688 | tf_op jit(solution)/shard_map/reduce_sum | solution.py:60
  190.1 8.3 %fusion.30 = f32[528,1024]{1,0:T(8,128)S(1)} fusion(bf16[528,2816]{1,0:T(8,128)(2,1)} %get-tuple-element.110, bf16[2816,1024]{1,0:T(8,128)(2,1)} %get-tuple-element.48), kind=kOutput, calls=%fused_computation.116 | convolution fusion | flops 3045064704 | bytes 10903552 | tf_op jit(solution)/shard_map/dot_general | solution.py:1681
  199.8 1.7 collective-permute-start.1
  201.5 5.6 %fusion.1 = f32[528,1024]{1,0:T(8,128)S(1)} fusion(bf16[528,2816]{1,0:T(8,128)(2,1)S(1)} %get-tuple-element.109, bf16[2,1024,2816]{2,1,0:T(8,128)(2,1)} %get-tuple-element.46), kind=kOutput, calls=%fused_computation.11 | convolution fusion | flops 3045064704 | bytes 10903552 | tf_op jit(solution)/shard_map/tf,df->td/dot_general | solution.py:1699
  207.2 3.9 multiply_reduce_fusion.4
  211.1 0.9 convert_reduce_fusion.3
  212.7 2.9 multiply_reduce_fusion.5
  215.6 3.3 convolution_convert_fusion.3.refs_3_
  218.9 6.6 %convolution_convert_fusion.refs_2_ = bf16[2816,1024]{1,0:T(8,128)(2,1)} fusion(bf16[528,2816]{1,0:T(8,128)(2,1)S(1)} %copy-done.6, bf16[528,1024]{1,0:T(8,128)(2,1)S(1)} %copy-done.13), kind=kOutput, calls=%fused_computation.19 | convolution fusion | flops 3047948288 | bytes 9822208 | tf_op jit(solution)/shard_map/tf,td->fd/dot_general | solution.py:1686
  225.5 7.0 %convolution_convert_fusion.1.refs_1_ = bf16[1024,2816]{1,0:T(8,128)(2,1)} fusion(bf16[528,1024]{1,0:T(8,128)(2,1)S(1)} %copy-done.10, bf16[528,2816]{1,0:T(8,128)(2,1)S(1)} %copy-done.5), kind=kOutput, calls=%fused_computation.20 | convolution fusion | flops 3047948288 | bytes 9822208 | tf_op jit(solution)/shard_map/td,tf->df/dot_general | solution.py:1697
  233.3 3.4 multiply_convert_fusion.2.refs_7_
  236.7 6.6 %convolution_convert_fusion.2.refs_0_ = bf16[1024,2816]{1,0:T(8,128)(2,1)} fusion(bf16[528,1024]{1,0:T(8,128)(2,1)S(1)} %copy-done.11, bf16[528,2816]{1,0:T(8,128)(2,1)S(1)} %copy-done.3), kind=kOutput, calls=%fused_computation.21 | convolution fusion | flops 3047948288 | bytes 9822208 | tf_op jit(solution)/shard_map/td,tf->df/dot_general | solution.py:1696
  243.3 196.8 %shard_map.221 = (f32[128,1408]{1,0:T(8,128)}, f32[128,1408]{1,0:T(8,128)}, f32[1408,128]{1,0:T(8,128)}, f32[512,128]{1,0:T(8,128)}, f32[128,512]{1,0:T(8,128)},...) custom-call(bf16[1024,2816]{1,0:T(8,128)(2,1)} %convolution_convert_, ...), custom_call_target="tpu_custom_call" | custom-call | tf_op jit(solution)/shard_map/pallas_call | solution.py:1561
  446.3 1.2 slice_bitcast_fusion.2
  447.7 2.1 copy.30
  449.7 1.7 slice_bitcast_fusion.1
  451.8 5.3 %copy.29 = f32[2,516,1024]{2,0,1:T(2,128)} copy(f32[2,516,1024]{2,1,0:T(8,128)S(1)} %convert_bitcast_fusion) | data formatting | bytes 8454144
  457.9 1.4 select_bitcast_fusion.1
  459.6 3.5 copy.28
  463.1 0.9 pad_maximum_fusion.1
  (135 shorter events, 19.3 us)
Async XLA Ops:
  3.9 2.4 copy-start.7
  8.5 2.0 copy-start.17
  8.5 2.7 copy-start.23
  8.5 2.7 copy-start.22
  8.5 3.4 copy-start.24
  8.5 3.4 copy-start.25
  152.3 3.0 copy-start
  153.4 3.4 copy-start.8
  155.3 5.5 %slice-start = ((s8[11534336]{0:T(1024)(128)(4,1)}), s8[4194304]{0:T(1024)(128)(4,1)S(1)}, s32[]{:S(2)}) async-start(s8[11534336]{0:T(1024)(128)(4,1)} %bitcast.82), calls=%async_computation | async-start | bytes 8388608
  156.7 4.1 slice-start.1
  156.8 4.1 slice-start.2
  160.8 3.3 copy-start.9
  190.1 11.4 %copy-start.4 = (bf16[528,2816]{1,0:T(8,128)(2,1)}, bf16[528,2816]{1,0:T(8,128)(2,1)S(1)}, u32[]{:S(2)}) copy-start(bf16[528,2816]{1,0:T(8,128)(2,1)S(1)} %get-tuple-element.109) | copy-start | bytes 8921092
  190.1 17.1 %copy-start.2 = (bf16[528,2816]{1,0:T(8,128)(2,1)}, bf16[528,2816]{1,0:T(8,128)(2,1)S(1)}, u32[]{:S(2)}) copy-start(bf16[528,2816]{1,0:T(8,128)(2,1)S(1)} %get-tuple-element.103) | copy-start | bytes 8921092
  198.3 8.8 %slice-start.3 = ((s8[11534336]{0:T(1024)(128)(4,1)}), s8[4194304]{0:T(1024)(128)(4,1)S(1)}, s32[]{:S(2)}) async-start(s8[11534336]{0:T(1024)(128)(4,1)} %bitcast.84), calls=%async_computation.3 | async-start | bytes 8388608
  198.9 44.4 %collective-permute-start = (bf16[516,1024]{1,0:T(8,128)(2,1)S(1)}, bf16[516,1024]{1,0:T(8,128)(2,1)}, u32[]{:S(2)}, u32[]{:S(2)}) collective-permute-start(bf16[516,1024]{1,0:T(8,128)(2,1)S(1)} %fusion.13), channel_id=1, source_target_pairs={{0,1},{1,0},{2,5},{3,4},{4,3},{5,2},{6,7},{7,6},{8,9},{9,8},{10,13... | collective-permute-start | bytes 3170312 | tf_op jit(solution)/shard_map/ppermute | solution.py:1683
  199.8 43.5 %collective-permute-start.1 = (bf16[516,1024]{1,0:T(8,128)(2,1)S(1)}, bf16[516,1024]{1,0:T(8,128)(2,1)}, u32[]{:S(2)}, u32[]{:S(2)}) collective-permute-start(bf16[516,1024]{1,0:T(8,128)(2,1)S(1)} %fusion.13), channel_id=1, source_target_pairs={{2,4},{4,2},{10,12},{12,10},{18,20},{20,18},{26,28},{28,26},{3,5},... | collective-permute-start | bytes 3170312 | tf_op jit(solution)/shard_map/ppermute | solution.py:1684
  201.4 5.7 %slice-start.4 = ((s8[11534336]{0:T(1024)(128)(4,1)}), s8[4194304]{0:T(1024)(128)(4,1)S(1)}, s32[]{:S(2)}) async-start(s8[11534336]{0:T(1024)(128)(4,1)} %bitcast.84), calls=%async_computation.4 | async-start | bytes 8388608
  201.4 5.7 %slice-start.5 = ((s8[11534336]{0:T(1024)(128)(4,1)}), s8[3145728]{0:T(1024)(128)(4,1)S(1)}, s32[]{:S(2)}) async-start(s8[11534336]{0:T(1024)(128)(4,1)} %bitcast.84), calls=%async_computation.5 | async-start | bytes 6291456
  207.2 3.9 copy-start.13
  212.0 3.6 copy-start.1
  215.6 3.3 copy-start.6
  218.9 6.6 %copy-start.5 = (bf16[528,2816]{1,0:T(8,128)(2,1)S(1)}, bf16[528,2816]{1,0:T(8,128)(2,1)}, u32[]{:S(2)}) copy-start(bf16[528,2816]{1,0:T(8,128)(2,1)} %copy-done.4) | copy-start | bytes 8921092
  218.9 6.6 %copy-start.10 = (bf16[528,1024]{1,0:T(8,128)(2,1)S(1)}, bf16[528,1024]{1,0:T(8,128)(2,1)}, u32[]{:S(2)}) copy-start(bf16[528,1024]{1,0:T(8,128)(2,1)} %copy-done.9) | copy-start | bytes 3244036
  233.3 3.4 copy-start.3
  233.3 3.4 copy-start.11
  440.0 7.5 %copy-start.14 = (f32[128,1408]{1,0:T(8,128)S(1)}, f32[128,1408]{1,0:T(8,128)}, u32[]{:S(2)}) copy-start(f32[128,1408]{1,0:T(8,128)} %get-tuple-element.69) | copy-start | bytes 2162692
  451.8 5.3 %copy-start.16 = (f32[1408,128]{1,0:T(8,128)S(1)}, f32[1408,128]{1,0:T(8,128)}, u32[]{:S(2)}) copy-start(f32[1408,128]{1,0:T(8,128)} %get-tuple-element.71) | copy-start | bytes 2162692
  459.6 3.5 copy-start.19
  459.6 3.5 copy-start.20
  459.6 3.5 copy-start.21
  459.6 4.5 copy-start.18
  (3 other events, 4.4 us)

commit v2 on v1

--- a/solution.py
+++ b/solution.py
@@ -1125,7 +1125,7 @@
         (COL, out_own, out_full, 0, out_rows, 320),
     ]
     starts = (0, 1, 2, 3, 4, 5, 6, 7, 8, 9, 10)
-    begins = (0, 0, 1, 2, 3, 4, 5, 6, 7, 8, 9)
+    begins = (0, 0, 0, 1, 2, 3, 4, 5, 6, 7, 8)
     jobs = [
         Gather(layers, links, kind, own, full, low, size, split, local_at())
         for kind, own, full, low, size, split in todo

time: 469 us -> 469 us (level)
  no operation moved by 1% of the time
where the time goes in v2:
time: 469 us; the launch traced here: 465 us
  Pallas kernels  336 us (72%)
  matrix products  66.5 us (14%)
  local copies, waits for them, and re-layouts  36.1 us (8%)
  other arithmetic  21.8 us (5%)
    pallas_call x1, Pallas kernels, back(): pl.pallas_call(functools.partial(back_kernel, layers, head_size, tokens_h...  197 us
    pallas_call x1, Pallas kernels, front(): pl.pallas_call(functools.partial(front_kernel, layers, head_size, grid_si...  139 us
    unnamed x85, local copies, waits for them, and re-layouts  17.5 us
    reduce_sum x2, other arithmetic, column_sum(): return jnp.sum(values.astype(jnp.float32), axis=0)  9.76 us
  transfers between devices with their start and end apart: 2, of which 0 were waited for; matrix products, arithmetic and copies ran while one was open for 9% of the time, Pallas kernels for 0%

profile of v2, /device:TPU:0, one launch (start us, length us, event | category | flops | bytes accessed | tf_op | source)
XLA Modules:
  0.0 464.6 jit_solution(17637447690644431711)
XLA Ops:
  1.6 2.2 copy.26
  3.9 1.5 pad.34.refs_5_
  6.9 1.6 pad.35.refs_6_
  8.5 1.0 copy.25
  9.5 0.9 pad.32.refs_3_
  12.5 139.1 %shard_map.220 = (bf16[128,1024]{1,0:T(8,128)(2,1)}, bf16[3,1024,1024]{2,1,0:T(8,128)(2,1)}, bf16[1024,1024]{1,0:T(8,128)(2,1)}, bf16[2,1024,2816]{2,1,0:T(8,128...) custom-call(bf16[16,512]{1,0:T(8,128)(2,1)} %fusion.21.refs_0_, ...), custom_call_target="tpu_custom_call" | custom-call | tf_op jit(solution)/shard_map/pallas_call | solution.py:1301
  152.8 1.9 reduce_sum.198
  155.1 1.1 fusion.28
  156.2 3.2 fusion.29
  160.2 3.3 fusion.7
  163.5 6.7 %fusion.27 = (f32[528]{0:T(1024)S(1)}, f32[528,2816]{1,0:T(8,128)S(1)}, f32[528,2816]{1,0:T(8,128)S(1)}) fusion(f32[2816]{0:T(1024)S(1)} %get-tuple-element.98, f32[528,2816]{1,0:T(8,128)S(1)} %fusion.7, f32[2816]{0:T(1024)S(1)} %get-tuple-element.99, bf16[528,1024]{1,0:T(8,128)(2,1)S(1)} %add_convert_fusion.1, bf16[2,1024,2816]{2,1,0:T(8,128)(2,1)} %get-tuple-element.46), kind=kOutput, calls=%fused_computation.113 | convolution fusion | flops 3056958976 | bytes 24715328 | tf_op jit(solution)/shard_map/dot_general | solution.py:1669
  171.4 9.2 %multiply_reduce_fusion = (f32[2816]{0:T(1024)S(1)}, f32[528]{0:T(1024)S(1)}, f32[528]{0:T(1024)S(1)}, f32[2816]{0:T(1024)S(1)}, f32[528,2816]{1,0:T(8,128)}) fusion(f32[528,2816]{1,0:T(8,128)S(1)} %get-tuple-element.107, f32[528]{0:T(1024)S(1)} %add_rsqrt_fusion, f32[528]{0:T(1024)S(1)} %broadcast_multiply_fusion.2, f32[2816]{0:T(1024)S(1)} %get-tuple-element.96, ...), kind=kOutput, calls=%fused_computation | convolution fusion | flops 3058439680 | bytes 18785536 | tf_op jit(solution)/shard_map/td,fd->tf/dot_general | solution.py:1687
  180.6 8.8 %convert_reduce_fusion.1 = (f32[2816]{0:T(1024)S(1)}, bf16[528,2816]{1,0:T(8,128)(2,1)S(1)}, f32[2816]{0:T(1024)S(1)}, bf16[528,2816]{1,0:T(8,128)(2,1)S(1)}, bf16[528,2816]{1,0:T(8,128)(2,1)}) fusion(f32[528,2816]{1,0:T(8,128)S(1)} %fusion.7, f32[2816]{0:T(1024)S(1)} %get-tuple-element.99, f32[528,2816]{1,0:T(8,128)S(1)} %get-tuple-element.126, ...), kind=kLoop, calls=%fused_computation.2 | loop fusion | flops 43112960 | bytes 32786688 | tf_op jit(solution)/shard_map/reduce_sum | solution.py:60
  189.5 8.3 %fusion.30 = f32[528,1024]{1,0:T(8,128)S(1)} fusion(bf16[528,2816]{1,0:T(8,128)(2,1)} %get-tuple-element.110, bf16[2816,1024]{1,0:T(8,128)(2,1)} %get-tuple-element.48), kind=kOutput, calls=%fused_computation.116 | convolution fusion | flops 3045064704 | bytes 10903552 | tf_op jit(solution)/shard_map/dot_general | solution.py:1681
  199.2 1.7 collective-permute-start.1
  200.9 5.6 %fusion.1 = f32[528,1024]{1,0:T(8,128)S(1)} fusion(bf16[528,2816]{1,0:T(8,128)(2,1)S(1)} %get-tuple-element.109, bf16[2,1024,2816]{2,1,0:T(8,128)(2,1)} %get-tuple-element.46), kind=kOutput, calls=%fused_computation.11 | convolution fusion | flops 3045064704 | bytes 10903552 | tf_op jit(solution)/shard_map/tf,df->td/dot_general | solution.py:1699
  206.6 3.9 multiply_reduce_fusion.4
  210.5 0.9 convert_reduce_fusion.3
  212.1 2.9 multiply_reduce_fusion.5
  215.0 3.3 convolution_convert_fusion.3.refs_3_
  218.3 6.6 %convolution_convert_fusion.refs_2_ = bf16[2816,1024]{1,0:T(8,128)(2,1)} fusion(bf16[528,2816]{1,0:T(8,128)(2,1)S(1)} %copy-done.6, bf16[528,1024]{1,0:T(8,128)(2,1)S(1)} %copy-done.13), kind=kOutput, calls=%fused_computation.19 | convolution fusion | flops 3047948288 | bytes 9822208 | tf_op jit(solution)/shard_map/tf,td->fd/dot_general | solution.py:1686
  224.9 7.0 %convolution_convert_fusion.1.refs_1_ = bf16[1024,2816]{1,0:T(8,128)(2,1)} fusion(bf16[528,1024]{1,0:T(8,128)(2,1)S(1)} %copy-done.10, bf16[528,2816]{1,0:T(8,128)(2,1)S(1)} %copy-done.5), kind=kOutput, calls=%fused_computation.20 | convolution fusion | flops 3047948288 | bytes 9822208 | tf_op jit(solution)/shard_map/td,tf->df/dot_general | solution.py:1697
  232.7 3.4 multiply_convert_fusion.2.refs_7_
  236.1 6.6 %convolution_convert_fusion.2.refs_0_ = bf16[1024,2816]{1,0:T(8,128)(2,1)} fusion(bf16[528,1024]{1,0:T(8,128)(2,1)S(1)} %copy-done.11, bf16[528,2816]{1,0:T(8,128)(2,1)S(1)} %copy-done.3), kind=kOutput, calls=%fused_computation.21 | convolution fusion | flops 3047948288 | bytes 9822208 | tf_op jit(solution)/shard_map/td,tf->df/dot_general | solution.py:1696
  242.7 197.1 %shard_map.221 = (f32[128,1408]{1,0:T(8,128)}, f32[128,1408]{1,0:T(8,128)}, f32[1408,128]{1,0:T(8,128)}, f32[512,128]{1,0:T(8,128)}, f32[128,512]{1,0:T(8,128)},...) custom-call(bf16[1024,2816]{1,0:T(8,128)(2,1)} %convolution_convert_, ...), custom_call_target="tpu_custom_call" | custom-call | tf_op jit(solution)/shard_map/pallas_call | solution.py:1561
  446.0 1.2 slice_bitcast_fusion.2
  447.4 2.1 copy.30
  449.4 1.7 slice_bitcast_fusion.1
  451.5 5.3 %copy.29 = f32[2,516,1024]{2,0,1:T(2,128)} copy(f32[2,516,1024]{2,1,0:T(8,128)S(1)} %convert_bitcast_fusion) | data formatting | bytes 8454144
  457.6 1.4 select_bitcast_fusion.1
  459.3 3.5 copy.28
  462.8 0.9 pad_maximum_fusion.1
  (135 shorter events, 19.3 us)
Async XLA Ops:
  3.9 2.4 copy-start.7
  8.5 2.0 copy-start.17
  8.5 2.7 copy-start.23
  8.5 2.7 copy-start.22
  8.5 3.4 copy-start.24
  8.5 3.4 copy-start.25
  151.7 3.0 copy-start
  152.8 3.4 copy-start.8
  154.7 5.5 %slice-start = ((s8[11534336]{0:T(1024)(128)(4,1)}), s8[4194304]{0:T(1024)(128)(4,1)S(1)}, s32[]{:S(2)}) async-start(s8[11534336]{0:T(1024)(128)(4,1)} %bitcast.82), calls=%async_computation | async-start | bytes 8388608
  156.1 4.1 slice-start.1
  156.2 4.1 slice-start.2
  160.2 3.3 copy-start.9
  189.5 11.4 %copy-start.4 = (bf16[528,2816]{1,0:T(8,128)(2,1)}, bf16[528,2816]{1,0:T(8,128)(2,1)S(1)}, u32[]{:S(2)}) copy-start(bf16[528,2816]{1,0:T(8,128)(2,1)S(1)} %get-tuple-element.109) | copy-start | bytes 8921092
  189.5 17.1 %copy-start.2 = (bf16[528,2816]{1,0:T(8,128)(2,1)}, bf16[528,2816]{1,0:T(8,128)(2,1)S(1)}, u32[]{:S(2)}) copy-start(bf16[528,2816]{1,0:T(8,128)(2,1)S(1)} %get-tuple-element.103) | copy-start | bytes 8921092
  197.7 8.8 %slice-start.3 = ((s8[11534336]{0:T(1024)(128)(4,1)}), s8[4194304]{0:T(1024)(128)(4,1)S(1)}, s32[]{:S(2)}) async-start(s8[11534336]{0:T(1024)(128)(4,1)} %bitcast.84), calls=%async_computation.3 | async-start | bytes 8388608
  198.3 44.4 %collective-permute-start = (bf16[516,1024]{1,0:T(8,128)(2,1)S(1)}, bf16[516,1024]{1,0:T(8,128)(2,1)}, u32[]{:S(2)}, u32[]{:S(2)}) collective-permute-start(bf16[516,1024]{1,0:T(8,128)(2,1)S(1)} %fusion.13), channel_id=1, source_target_pairs={{0,1},{1,0},{2,5},{3,4},{4,3},{5,2},{6,7},{7,6},{8,9},{9,8},{10,13... | collective-permute-start | bytes 3170312 | tf_op jit(solution)/shard_map/ppermute | solution.py:1683
  199.2 43.5 %collective-permute-start.1 = (bf16[516,1024]{1,0:T(8,128)(2,1)S(1)}, bf16[516,1024]{1,0:T(8,128)(2,1)}, u32[]{:S(2)}, u32[]{:S(2)}) collective-permute-start(bf16[516,1024]{1,0:T(8,128)(2,1)S(1)} %fusion.13), channel_id=1, source_target_pairs={{2,4},{4,2},{10,12},{12,10},{18,20},{20,18},{26,28},{28,26},{3,5},... | collective-permute-start | bytes 3170312 | tf_op jit(solution)/shard_map/ppermute | solution.py:1684
  200.8 5.7 %slice-start.4 = ((s8[11534336]{0:T(1024)(128)(4,1)}), s8[4194304]{0:T(1024)(128)(4,1)S(1)}, s32[]{:S(2)}) async-start(s8[11534336]{0:T(1024)(128)(4,1)} %bitcast.84), calls=%async_computation.4 | async-start | bytes 8388608
  200.8 5.7 %slice-start.5 = ((s8[11534336]{0:T(1024)(128)(4,1)}), s8[3145728]{0:T(1024)(128)(4,1)S(1)}, s32[]{:S(2)}) async-start(s8[11534336]{0:T(1024)(128)(4,1)} %bitcast.84), calls=%async_computation.5 | async-start | bytes 6291456
  206.6 3.9 copy-start.13
  211.5 3.6 copy-start.1
  215.0 3.3 copy-start.6
  218.3 6.6 %copy-start.5 = (bf16[528,2816]{1,0:T(8,128)(2,1)S(1)}, bf16[528,2816]{1,0:T(8,128)(2,1)}, u32[]{:S(2)}) copy-start(bf16[528,2816]{1,0:T(8,128)(2,1)} %copy-done.4) | copy-start | bytes 8921092
  218.3 6.6 %copy-start.10 = (bf16[528,1024]{1,0:T(8,128)(2,1)S(1)}, bf16[528,1024]{1,0:T(8,128)(2,1)}, u32[]{:S(2)}) copy-start(bf16[528,1024]{1,0:T(8,128)(2,1)} %copy-done.9) | copy-start | bytes 3244036
  232.7 3.4 copy-start.3
  232.7 3.4 copy-start.11
  439.7 7.5 %copy-start.14 = (f32[128,1408]{1,0:T(8,128)S(1)}, f32[128,1408]{1,0:T(8,128)}, u32[]{:S(2)}) copy-start(f32[128,1408]{1,0:T(8,128)} %get-tuple-element.69) | copy-start | bytes 2162692
  451.4 5.3 %copy-start.16 = (f32[1408,128]{1,0:T(8,128)S(1)}, f32[1408,128]{1,0:T(8,128)}, u32[]{:S(2)}) copy-start(f32[1408,128]{1,0:T(8,128)} %get-tuple-element.71) | copy-start | bytes 2162692
  459.3 3.5 copy-start.19
  459.3 3.5 copy-start.20
  459.3 3.5 copy-start.21
  459.3 4.5 copy-start.18
  (3 other events, 4.4 us)
